TPU v7x, 32 devices: a whole 2x2x4 slice. The times are simulated.
32 devices in a mesh: dp: 2 (over x), phase: 4 (over z), tensor: 4 (over y, core).
Axes of the slice: x: 2, y: 2, z: 4, core: 2. Of those that a mesh axis runs over, the one named last changes fastest.
Arguments:
- tokens: bfloat16 [2, 512, 8192], P('dp', 'phase', 'tensor'), may hold values from -6 to 6
- bc_proj: bfloat16 [2, 512, 2, 2048], P('dp', 'phase', None, 'tensor'), may hold values from -0.3984375 to 0.3984375
- step_sizes: bfloat16 [2, 64, 1024], P('dp', 'phase', 'tensor'), may hold values from 0.5 to 2
- decay_rates: float32 [128], P('tensor'), may hold values from 0.00024414062 to 0.02
- direct_weight: float32 [128], P('tensor'), may hold values from 0.5 to 1.5
- norm_gain: float32 [8192], P('tensor'), may hold values from 0.1 to 1.9
- routes: int32 [2, 64, 1], P('dp', 'phase'), may hold values from 0 to 1; in each aligned block of 16 rows (0 to 15, 16 to 31, ..., all dimensions but the last counted through in order) at most 16 rows name the same one
- segments: int32 [2, 1024], P('dp', 'phase'), may hold values from 0 to 3, never falling along the last dimension, each value on 1 to 512 neighbouring positions
Outputs:
- mixed: bfloat16 [2, 512, 8192], P('dp', 'phase', 'tensor')
Inputs may be any that keep to these rules, and one draw needn't show every extreme that they name: `routes`: no device sends more than 16 of its blocks to one data group. `segments`: document ids never fall along a row; each document covers 1 to 512 positions, and one covers exactly 512.
All inputs are finite; a program needn't handle non-finite values.
Results may differ from a plain program's by a relative error of at most 0.0075.
Values may be sent and summed in bfloat16 or wider, within the bound.
A program may use at most 128 MiB of HBM per device.

v0:
```python
import jax
import jax.numpy as jnp
from jax import lax
from jax.sharding import PartitionSpec as P

HEAD_FEATURES = 64
STATE_ENTRIES = 256
LOCAL_HEADS = 128
BLOCK = 8


EPSILON = 1e-05
PRECISE = lax.Precision.HIGHEST


def prefix(shard, axis, join, neutral):
    place = lax.axis_index(axis)
    gathered = jax.tree.map(
        lambda a, kind: lax.all_gather(a.astype(kind), axis),
        shard,
        (jnp.bfloat16, jnp.bfloat16, jnp.bfloat16, jnp.bfloat16),
    )
    state = jax.tree.map(lambda a, e: jnp.zeros_like(a) + jnp.asarray(e, a.dtype), shard, neutral)

    def one(step, state):
        return join(
            state,
            jax.tree.map(
                lambda a, own: lax.dynamic_index_in_dim(a, step, 0, False).astype(own.dtype),
                gathered,
                shard,
            ),
        )

    return lax.fori_loop(0, place, one, state)


def stretch_pass(
    carry_state, prior_id, x_stretch, b_stretch, c_stretch, dt_stretch, doc_ids, decay_rates
):
    span_len = x_stretch.shape[0]
    head_count = x_stretch.shape[1]
    groups = b_stretch.shape[1]
    per_group = head_count // groups
    log_decay = jnp.cumsum(-decay_rates[:, None] * dt_stretch, axis=1)
    x_groups = x_stretch.astype(jnp.float32).reshape(span_len, groups, per_group, -1)
    b_float = b_stretch.astype(jnp.float32)
    last_id = doc_ids[-1]
    tail_decay = (
        jnp.where(doc_ids[None, :] == last_id, jnp.exp(log_decay[:, -1:] - log_decay), 0.0)
        * dt_stretch
    )
    scaled = x_groups * tail_decay.T.reshape(span_len, groups, per_group)[..., None]
    update = jnp.einsum("jgkp,jgn->gkpn", scaled, b_float, precision=PRECISE).reshape(
        carry_state.shape
    )
    through = jnp.where(prior_id == last_id, jnp.exp(log_decay[:, -1]), 0.0)
    new_state = through[:, None, None] * carry_state + update
    positions = jnp.arange(span_len)
    same_doc = (doc_ids[:, None] == doc_ids[None, :]) & (positions[:, None] >= positions[None, :])
    gaps = jnp.minimum(log_decay[:, :, None] - log_decay[:, None, :], 0.0)
    decay_mat = jnp.where(same_doc[None], jnp.exp(gaps), 0.0) * dt_stretch[:, None, :]
    scores = jnp.einsum("ign,jgn->gij", c_stretch, b_stretch, preferred_element_type=jnp.float32)
    weights = decay_mat.reshape(groups, per_group, span_len, span_len) * scores[:, None]
    inside = jnp.einsum("gkij,jgkp->igkp", weights, x_groups, precision=PRECISE)
    state_groups = carry_state.reshape(
        groups, per_group, carry_state.shape[1], carry_state.shape[2]
    )
    carried = jnp.einsum(
        "ign,gkpn->igkp", c_stretch.astype(jnp.float32), state_groups, precision=PRECISE
    )
    keep_in = jnp.where(doc_ids[None, :] == prior_id, jnp.exp(log_decay), 0.0)
    result = inside + keep_in.T.reshape(span_len, groups, per_group)[..., None] * carried
    return (new_state, last_id, result.reshape(span_len, head_count, -1))


def local_scan(x_stretches, b_stretches, c_stretches, dt_stretches, doc_stretches, decay_rates):
    head_count = x_stretches.shape[2]

    def advance(carry, pieces):
        new_state, last_id, result = stretch_pass(
            carry[0], carry[1], pieces[0], pieces[1], pieces[2], pieces[3], pieces[4], decay_rates
        )
        return ((new_state, last_id), result)

    start_carry = (
        jnp.zeros((head_count, HEAD_FEATURES, STATE_ENTRIES), jnp.float32),
        jnp.array(-1.0, jnp.float32),
    )
    final_carry, scan_results = lax.scan(
        advance, start_carry, (x_stretches, b_stretches, c_stretches, dt_stretches, doc_stretches)
    )
    return (final_carry[0], scan_results)


def join_pieces(earlier, later):
    decay_one, state_one, first_one, last_one = earlier
    decay_two, state_two, first_two, last_two = later
    joined = (first_two == last_one) | (last_one < 0) | (first_two < 0)
    factor = jnp.where(joined, decay_two, 0.0)
    joined_state = factor[:, None, None] * state_one + state_two
    joined_decay = jnp.where(joined, decay_one * decay_two, 0.0)
    joined_first = jnp.where(first_one < 0, first_two, first_one)
    joined_last = jnp.where(last_two < 0, last_one, last_two)
    return (joined_decay, joined_state, joined_first, joined_last)


def per_device(
    tokens, bc_proj, step_sizes, decay_rates, direct_weight, norm_gain, routes, segments
):
    feature_width = tokens.shape[2]
    tok_count = tokens.shape[1]
    heads_dev = decay_rates.shape[0]
    groups_dev = bc_proj.shape[3] // STATE_ENTRIES
    per_group = heads_dev // groups_dev
    blocks = tok_count // BLOCK
    n_groups = lax.axis_size("dp")
    capacity = max(2, 2 * blocks // n_groups)
    slots = n_groups * capacity
    section = slots * BLOCK
    span_len = min(128, section)
    block_count = section // span_len
    targets = routes[0, :, 0]
    positions = jnp.arange(blocks)
    earlier = positions[:, None] > positions[None, :]
    slot_rank = jnp.sum((targets[:, None] == targets[None, :]) & earlier, axis=1)
    slot_index = targets * capacity + slot_rank
    placing = (slot_index[:, None] == jnp.arange(slots)[None, :]).astype(jnp.bfloat16)
    x_send = jnp.einsum(
        "bs,bf->sf",
        placing,
        tokens.reshape(blocks, BLOCK * feature_width),
        preferred_element_type=jnp.float32,
    )
    x_send = x_send.astype(jnp.bfloat16).reshape(n_groups, capacity, BLOCK, feature_width)
    bc_send = jnp.einsum(
        "bs,bf->sf",
        placing,
        bc_proj.reshape(blocks, BLOCK * 2 * groups_dev * STATE_ENTRIES),
        preferred_element_type=jnp.float32,
    )
    bc_send = bc_send.astype(jnp.bfloat16).reshape(
        n_groups, capacity, BLOCK, 2, groups_dev, STATE_ENTRIES
    )
    dt_send = jnp.einsum("bs,bf->sf", placing, step_sizes[0], preferred_element_type=jnp.float32)
    dt_send = dt_send.astype(jnp.bfloat16).reshape(n_groups, capacity, heads_dev * BLOCK)
    x_got, bc_got, dt_got = (
        lax.all_to_all(x_send, "dp", split_axis=0, concat_axis=0, tiled=True),
        lax.all_to_all(bc_send, "dp", split_axis=0, concat_axis=0, tiled=True),
        lax.all_to_all(dt_send, "dp", split_axis=0, concat_axis=0, tiled=True),
    )
    x_stretches = x_got.reshape(block_count, span_len, heads_dev, HEAD_FEATURES)
    b_stretches = bc_got[:, :, :, 0].reshape(block_count, span_len, groups_dev, STATE_ENTRIES)
    c_section = bc_got[:, :, :, 1].reshape(section, groups_dev, STATE_ENTRIES)
    c_stretches = c_section.reshape(block_count, span_len, groups_dev, STATE_ENTRIES)
    dt_section = (
        dt_got.reshape(slots, heads_dev, BLOCK)
        .astype(jnp.float32)
        .transpose(1, 0, 2)
        .reshape(heads_dev, section)
    )
    dt_stretches = dt_section.reshape(heads_dev, block_count, span_len).transpose(1, 0, 2)
    doc_ids = segments[0].astype(jnp.float32)
    doc_stretches = doc_ids.reshape(block_count, span_len)
    log_decay = jnp.cumsum(-decay_rates[:, None] * dt_section, axis=1)
    through = jnp.where(doc_ids[0] == doc_ids[-1], jnp.exp(log_decay[:, -1]), 0.0)
    identity = (
        jnp.ones((heads_dev,), jnp.float32),
        jnp.zeros((heads_dev, HEAD_FEATURES, STATE_ENTRIES), jnp.float32),
        jnp.array(-1.0, jnp.float32),
        jnp.array(-1.0, jnp.float32),
    )
    end_state, local_out = local_scan(
        x_stretches, b_stretches, c_stretches, dt_stretches, doc_stretches, decay_rates
    )
    incoming = prefix((through, end_state, doc_ids[0], doc_ids[-1]), "phase", join_pieces, identity)
    in_state = incoming[1]
    in_last = incoming[3]
    keep_in = jnp.where(doc_ids[None, :] == in_last, jnp.exp(log_decay), 0.0)
    state_groups = in_state.reshape(groups_dev, per_group, HEAD_FEATURES, STATE_ENTRIES)
    carried = jnp.einsum(
        "ign,gkpn->igkp", c_section.astype(jnp.float32), state_groups, precision=PRECISE
    )
    carried = carried.reshape(section, heads_dev, HEAD_FEATURES)
    combined = (
        local_out.reshape(section, heads_dev, HEAD_FEATURES) + keep_in.T[:, :, None] * carried
    )
    combined = combined + direct_weight[None, :, None] * x_got.reshape(
        section, heads_dev, HEAD_FEATURES
    ).astype(jnp.float32)
    y_section = combined.astype(jnp.bfloat16).reshape(section, feature_width)
    returned_rows = lax.all_to_all(
        y_section.reshape(n_groups, capacity, BLOCK * feature_width),
        "dp",
        split_axis=0,
        concat_axis=0,
        tiled=True,
    )
    restored = jnp.einsum(
        "bs,sf->bf",
        placing,
        returned_rows.reshape(slots, BLOCK * feature_width),
        preferred_element_type=jnp.float32,
    )
    restored = restored.astype(jnp.bfloat16).reshape(tok_count, feature_width)
    values = restored.astype(jnp.float32)
    square_sums = lax.psum(jnp.sum(values * values, axis=1), "tensor")
    mixed = (
        values
        * lax.rsqrt(square_sums / (LOCAL_HEADS * HEAD_FEATURES) + EPSILON)[:, None]
        * norm_gain
    ).astype(jnp.bfloat16)
    return mixed.reshape(1, tok_count, feature_width)


def solution(mesh):
    return jax.shard_map(
        per_device,
        mesh=mesh,
        in_specs=(
            P("dp", "phase", "tensor"),
            P("dp", "phase", None, "tensor"),
            P("dp", "phase", "tensor"),
            P("tensor"),
            P("tensor"),
            P("tensor"),
            P("dp", "phase", None),
            P("dp", "phase"),
        ),
        out_specs=P("dp", "phase", "tensor"),
        check_vma=False,
    )
```

profile of v0, /device:TPU:25, one launch (start us, length us, event | category | flops | bytes accessed | tf_op | source)
XLA Modules:
  0.0 227.0 jit_solution(8435461744368928688)
XLA Ops:
  9.0 3.2 %all-to-all-start = ((bf16[2,16,256]{2,1,0:T(8,128)(2,1)}), bf16[2,16,256]{2,1,0:T(8,128)(2,1)S(1)}, u32[]{:S(2)}, u32[]{:S(2)}) async-start(bf16[2,16,256]{2,1,0:T(8,128)(2,1)} %bitcast.9), calls=%async_computation | async-start | bytes 32768 | tf_op jit(solution)/shard_map/all_to_all | solution.py:150
  15.2 3.5 %all-to-all-start.2 = ((bf16[2,16,8,2,2,256]{5,4,3,2,1,0:T(2,128)(2,1)}), bf16[2,16,8,2,2,256]{5,4,3,2,1,0:T(2,128)(2,1)S(1)}, u32[]{:S(2)}, u32[]{:S(2)}) async-start(bf16[2,16,8,2,2,256]{5,4,3,2,1,0:T(2,128)(2,1)} %reshape.294), calls=%async_computation.2 | async-start | bytes 1048576 | tf_op jit(solution)/shard_map/all_to_all | solution.py:149
  20.8 4.3 %all-to-all-done.2 = bf16[2,16,8,2,2,256]{5,4,3,2,1,0:T(2,128)(2,1)S(1)} async-done(((bf16[2,16,8,2,2,256]{5,4,3,2,1,0:T(2,128)(2,1)}), bf16[2,16,8,2,2,256]{5,4,3,2,1,0:T(2,128)(2,1)S(1)}, u32[]{:S(2)}, u32[]{:S(2)}) %all-to-all-start.2) | async-done | bytes 524320 | tf_op jit(solution)/shard_map/all_to_all | solution.py:149
  25.2 3.6 %all-to-all-start.1 = ((bf16[2,16,8,2048]{3,2,1,0:T(8,128)(2,1)}), bf16[2,16,8,2048]{3,2,1,0:T(8,128)(2,1)S(1)}, u32[]{:S(2)}, u32[]{:S(2)}) async-start(bf16[2,16,8,2048]{3,2,1,0:T(8,128)(2,1)} %bitcast.66), calls=%async_computation.1 | async-start | bytes 2097152 | tf_op jit(solution)/shard_map/all_to_all | solution.py:148
  29.9 10.0 %all-to-all-done.1 = bf16[2,16,8,2048]{3,2,1,0:T(8,128)(2,1)S(1)} async-done(((bf16[2,16,8,2048]{3,2,1,0:T(8,128)(2,1)}), bf16[2,16,8,2048]{3,2,1,0:T(8,128)(2,1)S(1)}, u32[]{:S(2)}, u32[]{:S(2)}) %all-to-all-start.1) | async-done | bytes 1048608 | tf_op jit(solution)/shard_map/all_to_all | solution.py:148
  40.9 3.1 %reshape.292 = bf16[2,128,32,64]{3,2,1,0:T(8,128)(2,1)} reshape(bf16[2,16,8,2048]{3,2,1,0:T(8,128)(2,1)S(1)} %all-to-all-done.1) | data formatting | bytes 2097152 | tf_op jit(solution)/shard_map/reshape | solution.py:152
  44.1 3.3 %copy.54 = bf16[2,128,32,64]{1,3,2,0:T(8,128)(2,1)S(1)} copy(bf16[2,128,32,64]{3,2,1,0:T(8,128)(2,1)} %reshape.292) | data formatting | bytes 2097152
  47.4 24.9 %while.33 = (s32[]{:T(128)}, f32[32,64,256]{2,1,0:T(8,128)}, f32[]{:T(128)}, f32[2,128,32,64]{1,3,2,0:T(8,128)}, f32[2,128]{1,0:T(2,128)S(1)}, /*index=5*/f32[32...) while((s32[]{:T(128)}, f32[32,64,256]{2,1,0:T(8,128)}, ...), condition=%wide.region_3.4_spmd.clone, body=%wide.region_1.3_spmd.clone.sunk | while | flops 2035876096 | bytes 46125748 | solution.py:90
  62.6 3.5 %bitcast_add_fusion.2 = (f32[32,64,256]{2,1,0:T(8,128)}, f32[32,64,256]{2,1,0:T(8,128)S(1)}) fusion(f32[2,16,64,256]{3,2,1,0:T(8,128)S(1)} %fusion.81, f32[32]{0:T(128)S(1)} %broadcast_select_fusion.5, f32[32,64,256]{2,1,0:T(8,128)} %get-tuple-element.467, pred[]{:T(512)S(6)} %compare.3), kind=kLoop, calls=%fused_computation.3.clone.1 | loop fusion | flops 1572864 | bytes 8388737 | tf_op jit(solution)/shard_map/while/body/eval_jaxpr/add | solution.py:58
  72.4 2.8 %convert_element_type.146 = bf16[32,64,256]{2,1,0:T(8,128)(2,1)} convert(f32[32,64,256]{2,1,0:T(8,128)} %get-tuple-element.193) | non-fusion elementwise | flops 524288 | bytes 3145728 | tf_op jit(solution)/shard_map/convert_element_type | solution.py:19
  82.3 2.6 %mul.184 = f32[256,32,64]{2,1,0:T(8,128)} broadcast(f32[32]{0:T(128)S(1)} %copy-done.14), dimensions={1} | broadcast | bytes 2097280 | tf_op jit(solution)/shard_map/mul | solution.py:188
  84.9 4.4 %mul.185 = f32[2,16,16384]{2,1,0:T(8,128)} reshape(f32[256,32,64]{2,1,0:T(8,128)} %mul.184) | data formatting | bytes 4194304 | tf_op jit(solution)/shard_map/mul | solution.py:188
  89.3 6.5 %all-reduce.3 = (bf16[4]{0:T(256)(128)(2,1)S(1)}, bf16[128]{0:T(256)(128)(2,1)S(1)}, bf16[4]{0:T(256)(128)(2,1)S(1)}) all-reduce(bf16[4]{0:T(256)(128)(2,1)S(1)} %dynamic-update-slice, bf16[128]{0:T(256)(128)(2,1)S(1)} %dynamic-update-slice.1, bf16[4]{0:T(256)(128)(2,1)S(1)} %dynamic-update-slice.2), channel_id=2, replica_groups=mesh['dp'=2,'phase'=4,'tensor'=4] {'phase'}, use_global_device_ids=true, to_apply=%add | all-reduce | flops 136 | bytes 544 | tf_op jit(solution)/shard_map/all_gather | solution.py:19
  95.9 4.5 %copy.55 = f32[2,128,32,64]{3,2,1,0:T(8,128)} copy(f32[2,128,32,64]{1,3,2,0:T(8,128)S(1)} %copy-done.8) | data formatting | bytes 4194304 | tf_op jit(solution)/shard_map/while | solution.py:90
  100.5 4.0 %reshape.295 = f32[2,16,16384]{2,1,0:T(8,128)} reshape(f32[2,128,32,64]{3,2,1,0:T(8,128)} %copy.55) | data formatting | bytes 4194304 | tf_op jit(solution)/shard_map/reshape | solution.py:186
  106.0 50.5 %all-gather.6.cloned.1.call-done = bf16[128,64,256]{2,1,0:T(8,128)(2,1)} async-done(((bf16[32,64,256]{2,1,0:T(8,128)(2,1)}), bf16[128,64,256]{2,1,0:T(8,128)(2,1)}) %all-gather.6.cloned.1.call-update) | async-done | bytes 4194320 | tf_op jit(solution)/shard_map/all_gather | solution.py:19
  156.7 16.5 %while.32 = (s32[]{:T(128)}, f32[32,64,256]{2,1,0:T(8,128)S(1)}, f32[]{:T(128)}, s32[]{:T(128)}, bf16[4]{0:T(256)(128)(2,1)S(1)}, /*index=5*/bf16[4,32]{1,0:T(4,...) while((s32[]{:T(128)}, f32[32,64,256]{2,1,0:T(8,128)S(1)}, ...), condition=%wide.region_7.8_spmd, body=%wide.region_6.7_spmd.sunk | while | flops 1572940 | bytes 5243423 | solution.py:35
  175.7 5.5 %copy.60 = f32[256,2,16,64]{3,2,1,0:T(8,128)} copy(f32[256,2,16,64]{0,3,2,1:T(8,128)} %convolution_bitcast_fusion.1) | data formatting | bytes 4194304 | tf_op jit(solution)/shard_map/ign,gkpn->igkp/transpose | solution.py:181
  181.2 3.9 %reshape.298 = f32[2,16,16384]{2,1,0:T(8,128)} reshape(f32[256,2,16,64]{3,2,1,0:T(8,128)} %copy.60) | data formatting | bytes 4194304 | tf_op jit(solution)/shard_map/reshape | solution.py:184
  185.3 2.6 %mul.181 = f32[256,32,64]{2,1,0:T(8,128)} broadcast(f32[256,32]{1,0:T(8,128)S(1)} %copy.58), dimensions={0,1} | broadcast | bytes 2129920 | tf_op jit(solution)/shard_map/mul | solution.py:186
  187.9 4.0 %mul.182 = f32[2,16,16384]{2,1,0:T(8,128)} reshape(f32[256,32,64]{2,1,0:T(8,128)} %mul.181) | data formatting | bytes 4194304 | tf_op jit(solution)/shard_map/mul | solution.py:186
  191.9 4.2 %add_convert_fusion = bf16[2,16,16384]{2,1,0:T(8,128)(2,1)S(1)} fusion(f32[2,16,16384]{2,1,0:T(8,128)S(1)} %copy-done.5, f32[2,16,16384]{2,1,0:T(8,128)} %reshape.304, f32[2,16,16384]{2,1,0:T(8,128)} %reshape.295, f32[2,16,16384]{2,1,0:T(8,128)} %mul.182, f32[2,16,16384]{2,1,0:T(8,128)} %reshape.298), kind=kLoop, calls=%fused_computation.56 | loop fusion | flops 2621440 | bytes 11534336 | tf_op jit(solution)/shard_map/convert_element_type | solution.py:191
  196.1 15.4 %all_to_all.20 = bf16[2,16,16384]{2,1,0:T(8,128)(2,1)S(1)} all-to-all(bf16[2,16,16384]{2,1,0:T(8,128)(2,1)S(1)} %add_convert_fusion), channel_id=1, replica_groups=mesh['dp'=2,'phase'=4,'tensor'=4] {'dp'}, dimensions={0} | all-to-all | bytes 2097152 | tf_op jit(solution)/shard_map/all_to_all | solution.py:192
  212.2 6.7 %psum.7 = f32[128]{0:T(128)S(1)} all-reduce(f32[128]{0:T(128)S(1)} %reduce_sum.19), channel_id=1, replica_groups=mesh['dp'=2,'phase'=4,'tensor'=4] {'tensor'}, use_global_device_ids=true, to_apply=%region_9.10 | all-reduce | flops 128 | bytes 1024 | tf_op jit(solution)/shard_map/psum | solution.py:207
  (137 shorter events, 47.4 us)
Async XLA Ops:
  6.5 1.6 copy-start
  6.5 8.4 %copy-start.11 = (bf16[1,128,2048]{2,1,0:T(8,128)(2,1)S(1)}, bf16[1,128,2048]{2,1,0:T(8,128)(2,1)}, u32[]{:S(2)}) copy-start(bf16[1,128,2048]{2,1,0:T(8,128)(2,1)} %param.12) | copy-start | bytes 1572868
  9.0 6.2 %all-to-all-start = ((bf16[2,16,256]{2,1,0:T(8,128)(2,1)}), bf16[2,16,256]{2,1,0:T(8,128)(2,1)S(1)}, u32[]{:S(2)}, u32[]{:S(2)}) async-start(bf16[2,16,256]{2,1,0:T(8,128)(2,1)} %bitcast.9), calls=%async_computation | async-start | bytes 32768 | tf_op jit(solution)/shard_map/all_to_all | solution.py:150
  15.2 10.0 %all-to-all-start.2 = ((bf16[2,16,8,2,2,256]{5,4,3,2,1,0:T(2,128)(2,1)}), bf16[2,16,8,2,2,256]{5,4,3,2,1,0:T(2,128)(2,1)S(1)}, u32[]{:S(2)}, u32[]{:S(2)}) async-start(bf16[2,16,8,2,2,256]{5,4,3,2,1,0:T(2,128)(2,1)} %reshape.294), calls=%async_computation.2 | async-start | bytes 1048576 | tf_op jit(solution)/shard_map/all_to_all | solution.py:149
  19.2 9.6 %copy-start.15 = (f32[32]{0:T(128)S(1)}, f32[32]{0:T(128)}, u32[]{:S(2)}) copy-start(f32[32]{0:T(128)} %param.15) | copy-start | bytes 388
  19.3 9.6 %copy-start.13 = (s32[1,256]{1,0:T(1,128)S(1)}, s32[1,256]{1,0:T(1,128)}, u32[]{:S(2)}) copy-start(s32[1,256]{1,0:T(1,128)} %param.19) | copy-start | bytes 3076
  25.2 14.7 %all-to-all-start.1 = ((bf16[2,16,8,2048]{3,2,1,0:T(8,128)(2,1)}), bf16[2,16,8,2048]{3,2,1,0:T(8,128)(2,1)S(1)}, u32[]{:S(2)}, u32[]{:S(2)}) async-start(bf16[2,16,8,2048]{3,2,1,0:T(8,128)(2,1)} %bitcast.66), calls=%async_computation.1 | async-start | bytes 2097152 | tf_op jit(solution)/shard_map/all_to_all | solution.py:148
  28.7 127.8 %all-gather.6.cloned.1.call-start = ((), (), s32[]{:S(2)}) async-start(), calls=%async_computation.4 | async-start | bytes 5242880 | tf_op jit(solution)/shard_map/all_gather | solution.py:19
  29.3 14.8 %copy-start.9 = (f32[32,32,8]{0,2,1:T(8,128)}, f32[32,32,8]{0,2,1:T(8,128)S(1)}, u32[]{:S(2)}) copy-start(f32[32,32,8]{0,2,1:T(8,128)S(1)} %copy.50) | copy-start | bytes 98308
  47.4 1.9 copy-start.1
  55.5 1.6 copy-start.6
  56.6 1.9 copy-start.2
  57.2 1.3 copy-start.7
  59.1 1.9 copy-start.1
  68.8 1.6 copy-start.6
  69.9 1.9 copy-start.2
  70.4 1.3 copy-start.7
  72.3 5.9 %copy-start.16 = (u32[32]{0:T(128)S(1)}, u32[32]{0:T(128)}, u32[]{:S(2)}) copy-start(u32[32]{0:T(128)} %constant.86) | copy-start | bytes 388
  72.3 8.5 %copy-start.10 = (f32[32,32,8]{0,2,1:T(8,128)S(1)}, f32[32,32,8]{0,2,1:T(8,128)}, u32[]{:S(2)}) copy-start(f32[32,32,8]{0,2,1:T(8,128)} %copy-done.9) | copy-start | bytes 98308
  72.4 9.9 %copy-start.14 = (f32[32]{0:T(128)S(1)}, f32[32]{0:T(128)}, u32[]{:S(2)}) copy-start(f32[32]{0:T(128)} %param.16) | copy-start | bytes 388
  84.8 11.1 %copy-start.8 = (f32[2,128,32,64]{1,3,2,0:T(8,128)S(1)}, f32[2,128,32,64]{1,3,2,0:T(8,128)}, u32[]{:S(2)}) copy-start(f32[2,128,32,64]{1,3,2,0:T(8,128)} %get-tuple-element.192) | copy-start | bytes 6291460
  100.5 4.0 %copy-start.4 = (bf16[2,16,8,2048]{3,2,1,0:T(8,128)(2,1)S(1)}, bf16[2,16,8,2048]{3,2,1,0:T(8,128)(2,1)}, u32[]{:S(2)}) copy-start(bf16[2,16,8,2048]{3,2,1,0:T(8,128)(2,1)} %copy-done.3) | copy-start | bytes 3145732
  187.9 4.0 %copy-start.5 = (f32[2,16,16384]{2,1,0:T(8,128)S(1)}, f32[2,16,16384]{2,1,0:T(8,128)}, u32[]{:S(2)}) copy-start(f32[2,16,16384]{2,1,0:T(8,128)} %mul.185) | copy-start | bytes 6291460
  212.1 7.1 %copy-start.12 = (f32[2048]{0:T(1024)S(1)}, f32[2048]{0:T(1024)}, u32[]{:S(2)}) copy-start(f32[2048]{0:T(1024)} %param.17) | copy-start | bytes 24580
  (1 other events, 1.0 us)
Sparse Core Ops, SparseCore 0:
  75.3 81.1 all-gather.5
where the time goes:
time: 228 us; the launch traced here: 227 us
  waiting for transfers between devices  64.9 us (28%)
  local copies, waits for them, and re-layouts  58.5 us (26%)
  blocking collectives  28.7 us (13%)
  other arithmetic  23.2 us (10%)
  between operations  16.8 us (7%)
  matrix products  14 us (6%)
  loops' own time  10.5 us (5%)
  starting transfers between devices  10.4 us (5%)
    all_gather x1, waiting for transfers between devices, prefix(): lax.all_gather(a.astype(kind), axis)  50.5 us
    all_to_all x1, blocking collectives, per_device(): lax.all_to_all(y_section.reshape(n_groups, capacity, BLOCK * feature_widt...  15.4 us
    all_to_all x1, waiting for transfers between devices, per_device(): lax.all_to_all(x_send, 'dp', split_axis=0, concat_axis=0, tiled=True)  10 us
    unnamed x36, local copies, waits for them, and re-layouts  8.29 us
    another operation x1, loops' own time, prefix(): return lax.fori_loop(0, place, one, state)  7.99 us
    mul x2, local copies, waits for them, and re-layouts, per_device(): direct_weight[None, :, None]  6.99 us
    psum x1, blocking collectives, per_device(): square_sums = lax.psum(jnp.sum(values * values, axis=1), 'tensor')  6.73 us
    mul x2, local copies, waits for them, and re-layouts, per_device(): keep_in.T[:, :, None] * carried  6.57 us
  transfers between devices with their start and end apart: 4, of which 3 were waited for; matrix products, arithmetic and copies ran while one was open for 12% of the time, Pallas kernels for 0%

commit v1 on v0

v1 whole, which is shorter than its diff:
```python
import functools

import jax
import jax.numpy as jnp
from jax import lax
from jax.experimental import pallas as pl
from jax.experimental.pallas import tpu as pltpu
from jax.sharding import PartitionSpec as P

HEAD_FEATURES = 64
STATE_ENTRIES = 256
BLOCK = 8
EPSILON = 1e-05
LANES = 128
ROW_KEY = 1024.0
MESH = pl.DeviceIdType.MESH


def kernel(
    n_phase, n_tensor, total_features,
    x_ref, bc_ref, dt_ref, decay_ref, direct_ref, gain_ref, meta_ref,
    out_ref,
    xall, bcall, dtall, meta, metaprev, local, inside, hin, hout, ysend, ymine, sums, mysum,
    s_meta, r_meta, s_dt, r_dt, s_bc, r_bc, s_x, r_x, s_h, r_h, s_y, r_y, s_sum, r_sum,
):
    f32, bf16 = jnp.float32, jnp.bfloat16
    me, phase, place = lax.axis_index("dp"), lax.axis_index("phase"), lax.axis_index("tensor")
    other = 1 - me
    tok, width = x_ref.shape
    half = width // 2
    chunks = half // LANES
    n = STATE_ENTRIES
    partner = (other, phase, place)
    first, last = phase == 0, phase == n_phase - 1

    barrier = pltpu.get_barrier_semaphore()
    pl.semaphore_signal(barrier, inc=1, device_id=partner, device_id_type=MESH)
    for k in range(1, n_tensor):
        pl.semaphore_signal(
            barrier, inc=1, device_id=(me, phase, lax.rem(place + k, n_tensor)), device_id_type=MESH
        )

    @pl.when(phase > 0)
    def _():
        for d in (me, other):
            pl.semaphore_signal(barrier, inc=1, device_id=(d, phase - 1, place), device_id_type=MESH)

    @pl.when(phase < n_phase - 1)
    def _():
        for d in (me, other):
            pl.semaphore_signal(barrier, inc=1, device_id=(d, phase + 1, place), device_id_type=MESH)

    peers = n_tensor + 2 * jnp.minimum(phase, 1) + 2 * jnp.minimum(n_phase - 1 - phase, 1)
    pl.semaphore_wait(barrier, peers)

    def remote(src, dst, send, recv, device):
        return pltpu.make_async_remote_copy(
            src_ref=src, dst_ref=dst, send_sem=send, recv_sem=recv,
            device_id=device, device_id_type=MESH,
        )

    my_rows = pl.ds(pl.multiple_of(me * tok, tok), tok)
    other_rows = pl.ds(pl.multiple_of(other * tok, tok), tok)
    my_group = pl.ds(pl.multiple_of(me * n, n), n)
    other_group = pl.ds(pl.multiple_of(other * n, n), n)
    my_c = pl.ds(pl.multiple_of(2 * n + me * n, n), n)
    other_c = pl.ds(pl.multiple_of(2 * n + other * n, n), n)

    copies = [
        remote(meta_ref, meta.at[me], s_meta.at[0], r_meta.at[0], partner),
        remote(dt_ref.at[other], dtall.at[my_rows], s_dt, r_dt, partner),
        remote(bc_ref.at[:, other_group], bcall.at[my_rows, pl.ds(0, n)], s_bc.at[0], r_bc.at[0], partner),
        remote(bc_ref.at[:, other_c], bcall.at[my_rows, pl.ds(n, n)], s_bc.at[1], r_bc.at[1], partner),
    ]
    x_copies = [
        remote(
            x_ref.at[:, pl.ds(pl.multiple_of(other * half + c * LANES, LANES), LANES)],
            xall.at[my_rows, pl.ds(c * LANES, LANES)],
            s_x.at[c], r_x.at[c], partner,
        )
        for c in range(chunks)
    ]
    after = jnp.minimum(phase + 1, n_phase - 1)
    ahead = [
        remote(meta_ref, metaprev.at[me], s_meta.at[1 + i], r_meta.at[1 + i], (d, after, place))
        for i, d in enumerate((me, other))
    ]
    h_copies = [
        remote(hout.at[c], hin.at[c], s_h.at[c], r_h.at[c], (me, after, place)) for c in range(chunks)
    ]
    for copy in copies[:2]:
        copy.start()

    @pl.when(phase < n_phase - 1)
    def _():
        for copy in ahead:
            copy.start()

    for copy in copies[2:] + x_copies:
        copy.start()

    meta[me] = meta_ref[...]
    dtall[my_rows] = dt_ref[me]
    bcall[my_rows, pl.ds(0, n)] = bc_ref[:, my_group]
    bcall[my_rows, pl.ds(n, n)] = bc_ref[:, my_c]
    xall[my_rows, :] = x_ref[:, pl.ds(pl.multiple_of(me * half, half), half)]

    @pl.when(first)
    def _():
        metaprev[...] = jnp.full_like(metaprev, -(2.0**20))
        hin[...] = jnp.zeros_like(hin)

    copies[0].wait_recv()

    @pl.when(phase > 0)
    def _():
        for copy in ahead:
            copy.wait_recv()

    slots = lax.broadcasted_iota(jnp.int32, (tok, tok), 0).astype(f32)
    row_lanes, key_lanes, row_subl, key_subl = [], [], [], []
    for j in range(2):
        rows = meta[j, 0:1, :]
        places = jnp.where(slots == meta[j, 1:2, :], 1.0, 0.0).astype(bf16)
        found = [
            jnp.dot(meta[d].astype(bf16), places, preferred_element_type=f32)[2 + j : 3 + j, :]
            for d in range(2)
        ]
        key = rows * ROW_KEY + jnp.where(rows == 0.0, found[0], found[1])
        row_lanes.append(rows)
        key_lanes.append(key)
        row_subl.append(jnp.broadcast_to(rows, (tok, tok)).T)
        key_subl.append(jnp.broadcast_to(key, (tok, tok)).T)
    row_lane, key_lane = jnp.concatenate(row_lanes, 1), jnp.concatenate(key_lanes, 1)
    row_sub, key_sub = jnp.concatenate(row_subl, 0), jnp.concatenate(key_subl, 0)
    both = 2 * tok
    causal = lax.broadcasted_iota(jnp.int32, (both, both), 0) >= lax.broadcasted_iota(
        jnp.int32, (both, both), 1
    )
    row_sub2 = jnp.concatenate([row_sub, row_sub], 1)
    key_sub2 = jnp.concatenate([key_sub, key_sub], 1)
    same_row = jnp.where(causal & (row_sub2 == row_lane), 1.0, 0.0).astype(bf16)
    same_doc = jnp.where(causal & (key_sub2 == key_lane), 1.0, 0.0)

    ends = [meta[d, 3:4, tok - 1 : tok] for d in range(2)]
    befores = [metaprev[d, 3:4, tok - 1 : tok] for d in range(2)]
    through = [jnp.where(ends[d] == befores[d], 1.0, 0.0) for d in range(2)]

    copies[1].wait_recv()
    decay = decay_ref[me, 0:1, :]
    dt = dtall[...]
    log_decay = -decay * jnp.dot(same_row, dt, preferred_element_type=f32)
    grow = jnp.exp(-log_decay) * dt.astype(f32)
    shrink = jnp.exp(log_decay)
    picks = jnp.where(
        lax.broadcasted_iota(jnp.int32, (16, both), 0).astype(f32) == row_lane, 1.0, 0.0
    ).astype(bf16)
    whole = jnp.exp(-decay * jnp.dot(picks, dt, preferred_element_type=f32))

    copies[2].wait_recv()
    b_mat = bcall[:, 0:n]
    b_float = b_mat.astype(f32)
    b_both_t = jnp.concatenate(
        [
            jnp.where(key_sub2 == ends[d] + d * ROW_KEY, b_float, 0.0).T.astype(bf16)
            for d in range(2)
        ],
        0,
    )
    copies[3].wait_recv()
    c_mat = bcall[:, n : 2 * n]
    c_float = c_mat.astype(f32)
    c_both = jnp.concatenate(
        [
            jnp.where(key_sub2 == befores[d] + d * ROW_KEY, c_float, 0.0).astype(bf16)
            for d in range(2)
        ],
        1,
    )
    scores = lax.dot_general(c_mat, b_mat, (((1,), (1,)), ((), ())), preferred_element_type=f32)
    scores = (scores * same_doc).astype(bf16)

    def spread(a, c):
        low = lax.broadcasted_iota(jnp.int32, (a.shape[0], LANES), 1) < HEAD_FEATURES
        shape = (a.shape[0], LANES)
        return jnp.where(
            low,
            jnp.broadcast_to(a[:, 2 * c : 2 * c + 1], shape),
            jnp.broadcast_to(a[:, 2 * c + 1 : 2 * c + 2], shape),
        )

    for c in range(chunks):
        x_copies[c].wait_recv()
        cols = pl.ds(c * LANES, LANES)
        scaled = (xall[:, cols].astype(f32) * spread(grow, c)).astype(bf16)
        keep = spread(whole, c)
        update = jnp.dot(b_both_t, scaled, preferred_element_type=f32)
        for d in range(2):
            local[c, d * n : (d + 1) * n, :] = update[d * n : (d + 1) * n] * keep[d : d + 1]

        @pl.when(first)
        def _():
            hout[c] = local[c].astype(bf16)
            h_copies[c].start()

        inside[:, cols] = jnp.dot(scores, scaled, preferred_element_type=f32)

    squares = jnp.zeros((tok, LANES), f32)
    y_copies = []
    for c in range(chunks):
        cols = pl.ds(c * LANES, LANES)

        @pl.when(phase > 0)
        def _():
            h_copies[c].wait_recv()

        @pl.when((phase > 0) & (phase < n_phase - 1))
        def _():
            keep = spread(whole, c)
            for d in range(2):
                rows = slice(d * n, (d + 1) * n)
                hout[c, rows, :] = (
                    local[c, rows, :] + (keep[d : d + 1] * through[d]) * hin[c, rows, :].astype(f32)
                ).astype(bf16)
            h_copies[c].start()

        carried = jnp.dot(c_both, hin[c], preferred_element_type=f32)
        y = spread(shrink, c) * (inside[:, cols] + carried) + direct_ref[
            me, 0:1, c * LANES : (c + 1) * LANES
        ] * xall[:, cols].astype(f32)
        ysend[c] = y.astype(bf16)
        here = pl.ds(pl.multiple_of(me * half + c * LANES, LANES), LANES)
        copy = remote(ysend.at[c, other_rows], ymine.at[:, here], s_y.at[c], r_y.at[c], partner)
        copy.start()
        y_copies.append(copy)
        own = ysend[c, my_rows]
        ymine[:, here] = own
        own = own.astype(f32)
        squares = squares + own * own

    for c in range(chunks):
        y_copies[c].wait_recv()
        there = pl.ds(pl.multiple_of(other * half + c * LANES, LANES), LANES)
        got = ymine[:, there].astype(f32)
        squares = squares + got * got

    per_token = jnp.broadcast_to(jnp.sum(squares, axis=1, keepdims=True), (tok, tok)).T[0:8, :]
    mysum[...] = per_token
    sum_copies = []
    for k in range(1, n_tensor):
        copy = remote(
            mysum, sums.at[k - 1], s_sum.at[k - 1], r_sum.at[k - 1],
            (me, phase, lax.rem(place + k, n_tensor)),
        )
        copy.start()
        sum_copies.append(copy)
    total = per_token
    for k in range(1, n_tensor):
        sum_copies[k - 1].wait_recv()
        total = total + sums[k - 1]
    scale = lax.rsqrt(total[0:1, :] / total_features + EPSILON)
    scale = jnp.broadcast_to(scale, (tok, tok)).T
    for c in range(2 * chunks):
        cols = pl.ds(c * LANES, LANES)
        out_ref[:, cols] = (ymine[:, cols].astype(f32) * scale * gain_ref[0:1, cols]).astype(bf16)

    for copy in copies + x_copies + y_copies + sum_copies:
        copy.wait_send()

    @pl.when(phase < n_phase - 1)
    def _():
        for copy in ahead + h_copies:
            copy.wait_send()


def per_device(
    n_phase, n_tensor,
    tokens, bc_proj, step_sizes, decay_rates, direct_weight, norm_gain, routes, segments,
):
    tok, width = tokens.shape[1:]
    heads = decay_rates.shape[0]
    blocks = tok // BLOCK
    half = width // 2
    chunks = half // LANES
    n = STATE_ENTRIES
    f32, bf16 = jnp.float32, jnp.bfloat16

    targets = routes[0, :, 0]
    order = jnp.arange(blocks)
    earlier = order[:, None] > order[None, :]
    rank = jnp.sum((targets[:, None] == targets[None, :]) & earlier, axis=1)
    row = jnp.broadcast_to(targets[:, None], (blocks, BLOCK)).reshape(1, tok)
    slot = (rank[:, None] * BLOCK + jnp.arange(BLOCK)[None, :]).reshape(1, tok)
    meta = jnp.concatenate(
        [row, slot, segments.reshape(2, tok), jnp.zeros((4, tok), jnp.int32)], 0
    ).astype(f32)
    dt = step_sizes.reshape(blocks, 2, heads // 2, BLOCK).transpose(1, 0, 3, 2)
    dt = dt.reshape(2, tok, heads // 2)
    dt = jnp.pad(dt, ((0, 0), (0, 0), (0, LANES - heads // 2)))
    decay = jnp.pad(decay_rates.reshape(2, 1, heads // 2), ((0, 0), (0, 7), (0, LANES - heads // 2)))
    direct = jnp.broadcast_to(
        jnp.repeat(direct_weight, HEAD_FEATURES).reshape(2, 1, half), (2, 8, half)
    )
    dma = pltpu.SemaphoreType.DMA
    vmem = pltpu.VMEM
    out = pl.pallas_call(
        functools.partial(kernel, n_phase, n_tensor, float(n_tensor * width)),
        out_shape=jax.ShapeDtypeStruct((tok, width), bf16),
        in_specs=[pl.BlockSpec(memory_space=pltpu.VMEM)] * 7,
        out_specs=pl.BlockSpec(memory_space=pltpu.VMEM),
        scratch_shapes=[
            vmem((2 * tok, half), bf16),
            vmem((2 * tok, 2 * n), bf16),
            vmem((2 * tok, LANES), bf16),
            vmem((2, 8, tok), f32),
            vmem((2, 8, tok), f32),
            vmem((chunks, 2 * n, LANES), f32),
            vmem((2 * tok, half), f32),
            vmem((chunks, 2 * n, LANES), bf16),
            vmem((chunks, 2 * n, LANES), bf16),
            vmem((chunks, 2 * tok, LANES), bf16),
            vmem((tok, width), bf16),
            vmem((n_tensor - 1, 8, tok), f32),
            vmem((8, tok), f32),
            dma((3,)), dma((3,)), dma, dma, dma((2,)), dma((2,)),
            dma((chunks,)), dma((chunks,)), dma((chunks,)), dma((chunks,)),
            dma((chunks,)), dma((chunks,)), dma((n_tensor - 1,)), dma((n_tensor - 1,)),
        ],
        compiler_params=pltpu.CompilerParams(
            collective_id=0, has_side_effects=True, vmem_limit_bytes=40 * 2**20
        ),
    )(
        tokens.reshape(tok, width), bc_proj.reshape(tok, -1), dt, decay, direct,
        norm_gain.reshape(1, width), meta,
    )
    return out.reshape(1, tok, width)


def solution(mesh):
    return jax.shard_map(
        functools.partial(per_device, mesh.shape["phase"], mesh.shape["tensor"]),
        mesh=mesh,
        in_specs=(
            P("dp", "phase", "tensor"),
            P("dp", "phase", None, "tensor"),
            P("dp", "phase", "tensor"),
            P("tensor"),
            P("tensor"),
            P("tensor"),
            P("dp", "phase", None),
            P("dp", "phase"),
        ),
        out_specs=P("dp", "phase", "tensor"),
        check_vma=False,
    )
```

time: 228 us -> 52.3 us (0.23)
  waiting for transfers between devices: 64.9 us -> 0 us
  local copies, waits for them, and re-layouts: 58.5 us -> 3.03 us
  Pallas kernels: 0 us -> 48.6 us
  blocking collectives: 28.7 us -> 0 us
  other arithmetic: 23.2 us -> 0.33 us
  between operations: 16.8 us -> 0.12 us
  matrix products: 14 us -> 0 us
  loops' own time: 10.5 us -> 0 us
  starting transfers between devices: 10.4 us -> 0 us
    all_gather x1 -> x0, waiting for transfers between devices: 50.5 us -> none  [prefix(): lax.all_gather(a.astype(kind), axis)]
    pallas_call x0 -> x1, Pallas kernels: none -> 48.6 us  [per_device(): pl.pallas_call(functools.partial(kernel, n_phase, n_tensor, float(n_tenso...]
    all_to_all x1 -> x0, blocking collectives: 15.4 us -> none  [per_device(): lax.all_to_all(y_section.reshape(n_groups, capacity, BLOCK * feature_widt...]
    all_to_all x3 -> x0, waiting for transfers between devices: 14.4 us -> none  [the longest x1 10 us: per_device(): lax.all_to_all(x_send, 'dp', split_axis=0, concat_axis=0, tiled=True)]
    dot_general x13 -> x0, matrix products: 14 us -> none  [the longest x2 4.81 us: stretch_pass(): inside = jnp.einsum('gkij,jgkp->igkp', weights, x_groups, precision=PRECISE)]
    mul x6 -> x0, local copies, waits for them, and re-layouts: 13.8 us -> none  [the longest x2 6.99 us: per_device(): direct_weight[None, :, None]]
    reshape x6 -> x2, local copies, waits for them, and re-layouts: 13.6 us -> 0.17 us  [the longest x1 0.09 us: per_device(): row = jnp.broadcast_to(targets[:, None], (blocks, BLOCK)).reshape(1, tok)]
    add x6 -> x1, other arithmetic: 11 us -> 0.07 us  [per_device(): slot = (rank[:, None] * BLOCK + jnp.arange(BLOCK)[None, :]).reshape(1, tok)]
  transfers between devices with their start and end apart: 4 -> 0, of which waited for: 3 -> 0; matrix products, arithmetic and copies ran while one was open for 12% -> 0% of each run, Pallas kernels for 0% -> 0%
where the time goes in v1:
time: 52.3 us; the launch traced here: 52.1 us
  Pallas kernels  48.6 us (93%)
  local copies, waits for them, and re-layouts  3.03 us (6%)
    pallas_call x1, Pallas kernels, per_device(): pl.pallas_call(functools.partial(kernel, n_phase, n_tensor, float(n_tenso...  48.6 us
    unnamed x19, local copies, waits for them, and re-layouts  2.22 us

profile of v1, /device:TPU:25, one launch (start us, length us, event | category | flops | bytes accessed | tf_op | source)
XLA Modules:
  0.0 52.1 jit_solution(16581601171124403399)
XLA Ops:
  0.0 0.0 copy-start.4
  0.0 0.0 copy-start.3
  0.0 0.0 copy-start.2
  0.0 0.0 copy-start
  0.0 0.6 %copy-done.5 = s32[1,16,1]{1,2,0:T(1,128)S(1)} copy-done((s32[1,16,1]{1,2,0:T(1,128)S(1)}, s32[1,16,1]{1,2,0:T(1,128)}, u32[]{:S(2)}) %copy-start.5) | copy-done | bytes 88
  0.7 0.2 convert_reduce_fusion
  0.9 0.1 pad.13.clone
  0.9 0.0 copy-done.6
  0.9 0.1 reshape.66
  1.0 0.0 copy-done.7
  1.0 0.1 broadcast_in_dim.26
  1.1 0.1 iota_add_fusion
  1.2 0.1 add.30
  1.3 0.1 broadcast_in_dim.31
  1.3 0.1 reshape.68
  1.4 0.1 add_convert_fusion.meta_ref
  1.5 0.1 broadcast_in_dim.27
  1.6 0.1 broadcast_in_dim.28
  1.7 0.1 copy.14
  1.8 0.1 copy.15
  2.0 0.0 copy-start.1
  2.0 0.6 %copy-done.1 = f32[2048]{0:T(1024)S(1)} copy-done((f32[2048]{0:T(1024)S(1)}, f32[2048]{0:T(1024)}, u32[]{:S(2)}) %copy-start.1) | copy-done | bytes 8216
  2.7 48.6 %shard_map.82 = bf16[128,2048]{1,0:T(8,128)(2,1)S(1)} custom-call(bf16[128,2048]{1,0:T(8,128)(2,1)S(1)} %bitcast.15, bf16[128,1024]{1,0:T(8,128)(2,1)S(1)} %bitcast.14, bf16[2,128,128]{2,1,0:T(8,128)(2,1)S(1)} %pad.8.dt_ref, f32[2,8,128]{2,1,0:T(8,128)S(1)} %pad.9.decay_ref, f32[2,8,1024]{2,1,0:T(8,128)S(1)} %broadcast_in_dim.29.direct_ref, ...), custom_call_target="tpu_custom_call" | custom-call | tf_op jit(solution)/shard_map/pallas_call | solution.py:306
  51.3 0.8 %copy.19 = bf16[1,128,2048]{2,1,0:T(8,128)(2,1)} copy(bf16[1,128,2048]{2,1,0:T(8,128)(2,1)S(1)} %bitcast.13) | data formatting | bytes 1048576
  (13 shorter events, 0.1 us)
Async XLA Ops:
  0.0 0.7 %copy-start.5 = (s32[1,16,1]{1,2,0:T(1,128)S(1)}, s32[1,16,1]{1,2,0:T(1,128)}, u32[]{:S(2)}) copy-start(s32[1,16,1]{1,2,0:T(1,128)} %param.14) | copy-start | bytes 196
  0.0 0.9 %copy-start.6 = (f32[32]{0:T(128)S(1)}, f32[32]{0:T(128)}, u32[]{:S(2)}) copy-start(f32[32]{0:T(128)} %param.11) | copy-start | bytes 388
  0.0 1.0 %copy-start.7 = (f32[32]{0:T(128)S(1)}, f32[32]{0:T(128)}, u32[]{:S(2)}) copy-start(f32[32]{0:T(128)} %param.12) | copy-start | bytes 388
  0.0 1.4 %copy-start.4 = (s32[1,256]{1,0:T(1,128)S(1)}, s32[1,256]{1,0:T(1,128)}, u32[]{:S(2)}) copy-start(s32[1,256]{1,0:T(1,128)} %param.15) | copy-start | bytes 3076
  0.0 1.7 %copy-start.3 = (bf16[1,16,256]{2,1,0:T(8,128)(2,1)S(1)}, bf16[1,16,256]{2,1,0:T(8,128)(2,1)}, u32[]{:S(2)}) copy-start(bf16[1,16,256]{2,1,0:T(8,128)(2,1)} %param.10) | copy-start | bytes 24580
  0.0 1.9 %copy-start.2 = (bf16[1,128,2,512]{3,2,1,0:T(2,128)(2,1)S(1)}, bf16[1,128,2,512]{3,2,1,0:T(2,128)(2,1)}, u32[]{:S(2)}) copy-start(bf16[1,128,2,512]{3,2,1,0:T(2,128)(2,1)} %param.9) | copy-start | bytes 786436
  0.0 2.0 %copy-start = (bf16[1,128,2048]{2,1,0:T(8,128)(2,1)S(1)}, bf16[1,128,2048]{2,1,0:T(8,128)(2,1)}, u32[]{:S(2)}) copy-start(bf16[1,128,2048]{2,1,0:T(8,128)(2,1)} %param.8) | copy-start | bytes 1572868
  2.0 0.7 %copy-start.1 = (f32[2048]{0:T(1024)S(1)}, f32[2048]{0:T(1024)}, u32[]{:S(2)}) copy-start(f32[2048]{0:T(1024)} %param.13) | copy-start | bytes 24580

commit v2 on v1

v2 whole, which is shorter than its diff:
```python
import functools

import jax
import jax.numpy as jnp
from jax import lax
from jax.experimental import pallas as pl
from jax.experimental.pallas import tpu as pltpu
from jax.sharding import PartitionSpec as P

HEAD_FEATURES = 64
STATE_ENTRIES = 256
BLOCK = 8
EPSILON = 1e-05
LANES = 128
ROW_KEY = 1024.0
MESH = pl.DeviceIdType.MESH


def kernel(
    n_phase, n_tensor, total_features,
    x_ref, bc_ref, dt_ref, head_ref, meta_ref,
    y_ref, scale_ref,
    xall, bcall, dtall, meta, metaprev, local, xscaled, hin, hout, ysend, ymine, sums, mysum,
    s_meta, r_meta, s_dt, r_dt, s_bc, r_bc, s_x, r_x, s_h, r_h, s_y, r_y, s_sum, r_sum, s_own,
):
    f32, bf16 = jnp.float32, jnp.bfloat16
    me, phase, place = lax.axis_index("dp"), lax.axis_index("phase"), lax.axis_index("tensor")
    other = 1 - me
    tok, width = x_ref.shape
    half = width // 2
    chunks = half // LANES
    n = STATE_ENTRIES
    heads = dt_ref.shape[1]
    partner = (other, phase, place)
    first = phase == 0

    my_rows = pl.ds(pl.multiple_of(me * tok, tok), tok)
    other_rows = pl.ds(pl.multiple_of(other * tok, tok), tok)
    my_group = pl.ds(pl.multiple_of(me * n, n), n)
    other_group = pl.ds(pl.multiple_of(other * n, n), n)
    my_c = pl.ds(pl.multiple_of(2 * n + me * n, n), n)
    other_c = pl.ds(pl.multiple_of(2 * n + other * n, n), n)
    own_x = pltpu.make_async_copy(
        x_ref.at[:, pl.ds(pl.multiple_of(me * half, half), half)], xall.at[my_rows], s_own
    )
    own_x.start()

    barrier = pltpu.get_barrier_semaphore()
    pl.semaphore_signal(barrier, inc=1, device_id=partner, device_id_type=MESH)
    for k in range(1, n_tensor):
        pl.semaphore_signal(
            barrier, inc=1, device_id=(me, phase, lax.rem(place + k, n_tensor)), device_id_type=MESH
        )

    @pl.when(phase > 0)
    def _():
        for d in (me, other):
            pl.semaphore_signal(barrier, inc=1, device_id=(d, phase - 1, place), device_id_type=MESH)

    @pl.when(phase < n_phase - 1)
    def _():
        for d in (me, other):
            pl.semaphore_signal(barrier, inc=1, device_id=(d, phase + 1, place), device_id_type=MESH)

    peers = n_tensor + 2 * jnp.minimum(phase, 1) + 2 * jnp.minimum(n_phase - 1 - phase, 1)
    pl.semaphore_wait(barrier, peers)

    def remote(src, dst, send, recv, device):
        return pltpu.make_async_remote_copy(
            src_ref=src, dst_ref=dst, send_sem=send, recv_sem=recv,
            device_id=device, device_id_type=MESH,
        )

    copies = [
        remote(meta_ref, meta.at[me], s_meta.at[0], r_meta.at[0], partner),
        remote(dt_ref.at[other], dtall.at[me], s_dt, r_dt, partner),
        remote(bc_ref.at[:, other_group], bcall.at[my_rows, pl.ds(0, n)], s_bc.at[0], r_bc.at[0], partner),
        remote(bc_ref.at[:, other_c], bcall.at[my_rows, pl.ds(n, n)], s_bc.at[1], r_bc.at[1], partner),
    ]
    x_copies = [
        remote(
            x_ref.at[:, pl.ds(pl.multiple_of(other * half + c * LANES, LANES), LANES)],
            xall.at[my_rows, pl.ds(c * LANES, LANES)],
            s_x.at[c], r_x.at[c], partner,
        )
        for c in range(chunks)
    ]
    after = jnp.minimum(phase + 1, n_phase - 1)
    ahead = [
        remote(meta_ref, metaprev.at[me], s_meta.at[1 + i], r_meta.at[1 + i], (d, after, place))
        for i, d in enumerate((me, other))
    ]
    h_copies = [
        [
            remote(
                hout.at[c, pl.ds(d * n, n)], hin.at[c, pl.ds(d * n, n)],
                s_h.at[2 * c + d], r_h.at[2 * c + d], (me, after, place),
            )
            for d in range(2)
        ]
        for c in range(chunks)
    ]
    for copy in copies[:3] + x_copies[:4] + copies[3:] + x_copies[4:]:
        copy.start()

    @pl.when(phase < n_phase - 1)
    def _():
        for copy in ahead:
            copy.start()

    meta[me] = meta_ref[...]
    dtall[me] = dt_ref[me]
    bcall[my_rows, pl.ds(0, n)] = bc_ref[:, my_group]
    bcall[my_rows, pl.ds(n, n)] = bc_ref[:, my_c]

    @pl.when(first)
    def _():
        metaprev[...] = jnp.full_like(metaprev, -(2.0**20))
        hin[...] = jnp.zeros_like(hin)

    both = 2 * tok
    at_row = lax.broadcasted_iota(jnp.int32, (both, both), 0)
    at_col = lax.broadcasted_iota(jnp.int32, (both, both), 1)
    causal = at_row >= at_col
    unit = jnp.where(at_row == at_col, 1.0, 0.0).astype(bf16)
    slots = lax.broadcasted_iota(jnp.int32, (tok, tok), 0).astype(f32)

    copies[0].wait_recv()

    row_lanes, key_lanes, row_subl, key_subl = [], [], [], []
    for j in range(2):
        rows = meta[j, 0:1, :]
        places = jnp.where(slots == meta[j, 1:2, :], 1.0, 0.0).astype(bf16)
        found = [
            jnp.dot(meta[d].astype(bf16), places, preferred_element_type=f32)[2 + j : 3 + j, :]
            for d in range(2)
        ]
        key = rows * ROW_KEY + jnp.where(rows == 0.0, found[0], found[1])
        row_lanes.append(rows)
        key_lanes.append(key)
        row_subl.append(jnp.broadcast_to(rows, (tok, tok)).T)
        key_subl.append(jnp.broadcast_to(key, (tok, tok)).T)
    row_lane, key_lane = jnp.concatenate(row_lanes, 1), jnp.concatenate(key_lanes, 1)
    row_sub, key_sub = jnp.concatenate(row_subl, 0), jnp.concatenate(key_subl, 0)
    row_sub2 = jnp.concatenate([row_sub, row_sub], 1)
    key_sub2 = jnp.concatenate([key_sub, key_sub], 1)
    same_row = jnp.where(causal & (row_sub2 == row_lane), 1.0, 0.0).astype(bf16)
    picks = jnp.where(
        lax.broadcasted_iota(jnp.int32, (16, both), 0).astype(f32) == row_lane, 1.0, 0.0
    ).astype(bf16)
    ends = [meta[d, 3:4, tok - 1 : tok] for d in range(2)]

    copies[1].wait_recv()
    decay = head_ref[me, 0:1, 0:heads]
    dt_lanes = jnp.concatenate([dtall[0], dtall[1]], 1)
    steps = lax.dot_general(
        jnp.concatenate([same_row, unit, picks], 0), dt_lanes,
        (((1,), (1,)), ((), ())), preferred_element_type=f32,
    )
    log_decay = -decay * steps[0:both]
    grow = jnp.exp(-log_decay) * steps[both : 2 * both]
    shrink = jnp.exp(log_decay)
    whole = jnp.exp(-decay * steps[2 * both : 2 * both + 8])

    copies[2].wait_recv()
    b_mat = bcall[:, 0:n]
    b_float = b_mat.astype(f32)
    b_both_t = jnp.concatenate(
        [
            jnp.where(key_sub2 == ends[d] + d * ROW_KEY, b_float, 0.0).T.astype(bf16)
            for d in range(2)
        ],
        0,
    )

    def spread(a, c):
        low = lax.broadcasted_iota(jnp.int32, (a.shape[0], LANES), 1) < HEAD_FEATURES
        shape = (a.shape[0], LANES)
        return jnp.where(
            low,
            jnp.broadcast_to(a[:, 2 * c : 2 * c + 1], shape),
            jnp.broadcast_to(a[:, 2 * c + 1 : 2 * c + 2], shape),
        )

    own_x.wait()
    for c in range(chunks):
        x_copies[c].wait_recv()
        cols = pl.ds(c * LANES, LANES)
        scaled = (xall[:, cols].astype(f32) * spread(grow, c)).astype(bf16)
        xscaled[:, cols] = scaled
        keep = spread(whole, c)
        update = jnp.dot(b_both_t, scaled, preferred_element_type=f32)
        update = jnp.concatenate(
            [update[d * n : (d + 1) * n] * keep[d : d + 1] for d in range(2)], 0
        )

        @pl.when(first)
        def _():
            hout[c] = update.astype(bf16)
            for d in range(2):
                h_copies[c][d].start()

        @pl.when(phase > 0)
        def _():
            local[c] = update

    @pl.when(phase > 0)
    def _():
        for copy in ahead:
            copy.wait_recv()

    befores = [metaprev[d, 3:4, tok - 1 : tok] for d in range(2)]
    through = [jnp.where(ends[d] == befores[d], 1.0, 0.0) for d in range(2)]
    copies[3].wait_recv()
    c_mat = bcall[:, n : 2 * n]
    c_float = c_mat.astype(f32)
    c_both = jnp.concatenate(
        [
            jnp.where(key_sub2 == befores[d] + d * ROW_KEY, c_float, 0.0).astype(bf16)
            for d in range(2)
        ],
        1,
    )
    scores = lax.dot_general(c_mat, b_mat, (((1,), (1,)), ((), ())), preferred_element_type=f32)
    scores = jnp.where(causal & (key_sub2 == key_lane), scores, 0.0).astype(bf16)

    squares = jnp.zeros((tok, LANES), f32)
    y_copies = []
    for c in range(chunks):
        cols = pl.ds(c * LANES, LANES)
        inside = jnp.dot(scores, xscaled[:, cols], preferred_element_type=f32)
        decayed = spread(shrink, c)
        direct = spread(head_ref[me, 1:2, :], c) * xall[:, cols].astype(f32)
        keep = spread(whole, c)
        for d in range(2):
            rows = pl.ds(d * n, n)

            @pl.when(phase > 0)
            def _():
                h_copies[c][d].wait_recv()

            @pl.when((phase > 0) & (phase < n_phase - 1))
            def _():
                hout[c, rows, :] = (
                    local[c, rows, :] + (keep[d : d + 1] * through[d]) * hin[c, rows, :].astype(f32)
                ).astype(bf16)
                h_copies[c][d].start()

        carried = jnp.dot(c_both, hin[c], preferred_element_type=f32)
        ysend[c] = (decayed * (inside + carried) + direct).astype(bf16)
        here = pl.ds(pl.multiple_of(me * half + c * LANES, LANES), LANES)
        copy = remote(ysend.at[c, other_rows], ymine.at[:, here], s_y.at[c], r_y.at[c], partner)
        copy.start()
        y_copies.append(copy)
        own = ysend[c, my_rows]
        y_ref[:, here] = own
        own = own.astype(f32)
        squares = squares + own * own

    for c in range(chunks):
        y_copies[c].wait_recv()
        there = pl.ds(pl.multiple_of(other * half + c * LANES, LANES), LANES)
        got = ymine[:, there]
        y_ref[:, there] = got
        got = got.astype(f32)
        squares = squares + got * got

    per_token = jnp.broadcast_to(jnp.sum(squares, axis=1, keepdims=True), (tok, tok)).T[0:8, :]
    mysum[...] = per_token
    sum_copies = []
    for k in range(1, n_tensor):
        copy = remote(
            mysum, sums.at[k - 1], s_sum.at[k - 1], r_sum.at[k - 1],
            (me, phase, lax.rem(place + k, n_tensor)),
        )
        copy.start()
        sum_copies.append(copy)
    total = per_token
    for copy in copies + x_copies + y_copies:
        copy.wait_send()

    @pl.when(phase < n_phase - 1)
    def _():
        for copy in ahead + [copy for pair in h_copies for copy in pair]:
            copy.wait_send()

    for k in range(1, n_tensor):
        sum_copies[k - 1].wait_recv()
        total = total + sums[k - 1]
    scale_ref[...] = lax.rsqrt(total / total_features + EPSILON)
    for copy in sum_copies:
        copy.wait_send()


def per_device(
    n_phase, n_tensor,
    tokens, bc_proj, step_sizes, decay_rates, direct_weight, norm_gain, routes, segments,
):
    tok, width = tokens.shape[1:]
    heads = decay_rates.shape[0] // 2
    blocks = tok // BLOCK
    half = width // 2
    chunks = half // LANES
    n = STATE_ENTRIES
    f32, bf16 = jnp.float32, jnp.bfloat16

    targets = routes[0, :, 0]
    order = jnp.arange(blocks)
    earlier = order[:, None] > order[None, :]
    rank = jnp.sum((targets[:, None] == targets[None, :]) & earlier, axis=1)
    row = jnp.broadcast_to(targets[:, None], (blocks, BLOCK)).reshape(1, tok)
    slot = (rank[:, None] * BLOCK + jnp.arange(BLOCK)[None, :]).reshape(1, tok)
    meta = jnp.concatenate(
        [row, slot, segments.reshape(2, tok), jnp.zeros((4, tok), jnp.int32)], 0
    ).astype(f32)
    dt = step_sizes.reshape(blocks, 2, heads, BLOCK).transpose(1, 2, 0, 3).reshape(2, heads, tok)
    by_head = jnp.stack([decay_rates.reshape(2, heads), direct_weight.reshape(2, heads)], 1)
    by_head = jnp.pad(by_head, ((0, 0), (0, 6), (0, LANES - heads)))
    dma = pltpu.SemaphoreType.DMA
    vmem = pltpu.VMEM
    y, scale = pl.pallas_call(
        functools.partial(kernel, n_phase, n_tensor, float(n_tensor * width)),
        out_shape=[
            jax.ShapeDtypeStruct((tok, width), bf16),
            jax.ShapeDtypeStruct((8, tok), f32),
        ],
        in_specs=[pl.BlockSpec(memory_space=pltpu.HBM)]
        + [pl.BlockSpec(memory_space=pltpu.VMEM)] * 4,
        out_specs=[pl.BlockSpec(memory_space=pltpu.VMEM)] * 2,
        scratch_shapes=[
            vmem((2 * tok, half), bf16),
            vmem((2 * tok, 2 * n), bf16),
            vmem((2, heads, tok), bf16),
            vmem((2, 8, tok), f32),
            vmem((2, 8, tok), f32),
            vmem((chunks, 2 * n, LANES), f32),
            vmem((2 * tok, half), bf16),
            vmem((chunks, 2 * n, LANES), bf16),
            vmem((chunks, 2 * n, LANES), bf16),
            vmem((chunks, 2 * tok, LANES), bf16),
            vmem((tok, width), bf16),
            vmem((n_tensor - 1, 8, tok), f32),
            vmem((8, tok), f32),
            dma((3,)), dma((3,)), dma, dma, dma((2,)), dma((2,)),
            dma((chunks,)), dma((chunks,)), dma((2 * chunks,)), dma((2 * chunks,)),
            dma((chunks,)), dma((chunks,)), dma((n_tensor - 1,)), dma((n_tensor - 1,)), dma,
        ],
        compiler_params=pltpu.CompilerParams(
            collective_id=0, has_side_effects=True, vmem_limit_bytes=40 * 2**20
        ),
    )(tokens.reshape(tok, width), bc_proj.reshape(tok, -1), dt, by_head, meta)
    mixed = y.astype(f32) * scale[0][:, None] * norm_gain[None, :]
    return mixed.astype(bf16).reshape(1, tok, width)


def solution(mesh):
    return jax.shard_map(
        functools.partial(per_device, mesh.shape["phase"], mesh.shape["tensor"]),
        mesh=mesh,
        in_specs=(
            P("dp", "phase", "tensor"),
            P("dp", "phase", None, "tensor"),
            P("dp", "phase", "tensor"),
            P("tensor"),
            P("tensor"),
            P("tensor"),
            P("dp", "phase", None),
            P("dp", "phase"),
        ),
        out_specs=P("dp", "phase", "tensor"),
        check_vma=False,
    )
```

time: 52.3 us -> 53.2 us (1.017)
  other arithmetic: 0.33 us -> 2.75 us
  Pallas kernels: 48.6 us -> 46.7 us
    pallas_call x1, Pallas kernels: 48.6 us -> 46.7 us  [per_device(): pl.pallas_call(functools.partial(kernel, n_phase, n_tensor, float(n_tenso...]
    another operation x0 -> x2, local copies, waits for them, and re-layouts: none -> 1.47 us  [per_device(): jnp.stack([decay_rates.reshape(2, heads), direct_weight.reshape(2, heads)...]
    unnamed x19 -> x8, local copies, waits for them, and re-layouts: 2.22 us -> 0.88 us
    reshape x0 -> x1, other arithmetic: none -> 0.98 us  [per_device(): return mixed.astype(bf16).reshape(1, tok, width)]
    reduce_sum x1, other arithmetic: 0.18 us -> 0.93 us  [per_device(): rank = jnp.sum((targets[:, None] == targets[None, :]) & earlier, axis=1)]
    convert_element_type x1, other arithmetic: 0.07 us -> 0.75 us  [per_device(): meta = jnp.concatenate([row, slot, segments.reshape(2, tok), jnp.zeros((4...]
    broadcast_in_dim x1, local copies, waits for them, and re-layouts: 0.07 us -> 0.73 us  [per_device(): row = jnp.broadcast_to(targets[:, None], (blocks, BLOCK)).reshape(1, tok)]
where the time goes in v2:
time: 53.2 us; the launch traced here: 53 us
  Pallas kernels  46.7 us (88%)
  local copies, waits for them, and re-layouts  3.54 us (7%)
  other arithmetic  2.75 us (5%)
    pallas_call x1, Pallas kernels, per_device(): pl.pallas_call(functools.partial(kernel, n_phase, n_tensor, float(n_tenso...  46.7 us
    another operation x2, local copies, waits for them, and re-layouts, per_device(): jnp.stack([decay_rates.reshape(2, heads), direct_weight.reshape(2, heads)...  1.47 us

profile of v2, /device:TPU:25, one launch (start us, length us, event | category | flops | bytes accessed | tf_op | source)
XLA Modules:
  0.0 53.0 jit_solution(14584703297985391840)
XLA Ops:
  0.0 0.0 copy-start.1
  0.0 0.0 copy-start
  0.0 0.9 %convert_reduce_fusion = s32[16]{0:T(128)S(1)} fusion(s32[16]{0:T(128)} %bitcast.24), kind=kLoop, calls=%fused_computation.6 | loop fusion | flops 1264 | bytes 128 | tf_op jit(solution)/shard_map/reduce_sum | solution.py:310
  0.9 0.1 pad.8.clone
  1.0 0.7 %stack_reshape.6 = f32[2,1,16]{2,0,1:T(2,128)S(1)} reshape(f32[32]{0:T(128)} %param.11) | data formatting | bytes 256 | tf_op jit(solution)/shard_map/stack;reshape | solution.py:317
  1.8 0.7 %stack_reshape.7 = f32[2,1,16]{2,0,1:T(2,128)S(1)} reshape(f32[32]{0:T(128)} %param.12) | data formatting | bytes 256 | tf_op jit(solution)/shard_map/stack;reshape | solution.py:317
  2.5 0.1 iota_add_fusion
  2.6 0.1 add.28
  2.7 0.7 %broadcast_in_dim.7 = s32[16,8]{1,0:T(8,128)S(1)} broadcast(s32[16]{0:T(128)} %bitcast.25), dimensions={0} | broadcast | bytes 576 | tf_op jit(solution)/shard_map/broadcast_in_dim | solution.py:311
  3.4 0.1 reshape.56
  3.5 0.8 %add_convert_fusion.meta_ref = f32[8,128]{1,0:T(8,128)S(1)} fusion(s32[2,128]{1,0:T(2,128)} %bitcast.23, s32[1,128]{1,0:T(1,128)S(1)} %add.28, s32[1,128]{1,0:T(1,128)S(1)} %reshape.56, s32[8]{0:T(128)S(1)} %pad.8.clone), kind=kLoop, calls=%fused_computation.9 | loop fusion | flops 4096 | bytes 6176 | tf_op jit(solution)/shard_map/convert_element_type | solution.py:315
  4.2 0.8 %copy.17 = bf16[1,16,256]{1,2,0:T(8,128)(2,1)S(1)} copy(bf16[1,16,256]{2,1,0:T(8,128)(2,1)} %param.10) | data formatting | bytes 16384 | tf_op args[2]
  5.1 0.1 copy.18
  5.2 0.1 copy.21.dt_ref
  5.3 0.0 copy-done.1
  5.3 0.1 copy.22
  5.3 0.0 copy-done
  5.3 0.0 copy-start.2
  5.3 46.7 %shard_map.82 = (bf16[128,2048]{1,0:T(8,128)(2,1)S(1)}, f32[8,128]{1,0:T(8,128)S(1)}) custom-call(bf16[128,2048]{1,0:T(8,128)(2,1)S(1)} %bitcast.17, bf16[128,1024]{1,0:T(8,128)(2,1)S(1)} %bitcast.16, bf16[2,16,128]{2,1,0:T(8,128)(2,1)S(1)} %copy.21.dt_ref, f32[2,8,128]{2,1,0:T(8,128)S(1)} %select_maximum_fusion.head_ref, f32[8,128]{1,0:T(8,128)S(1)} %add_convert_fusion.meta_ref), custom_call_target="tpu_custom_call" | custom-call | tf_op jit(solution)/shard_map/pallas_call | solution.py:321
  52.0 0.0 copy-done.2
  52.0 1.0 %fusion = bf16[1,128,2048]{2,1,0:T(8,128)(2,1)} fusion(bf16[128,2048]{1,0:T(8,128)(2,1)S(1)} %get-tuple-element.7, f32[2048]{0:T(1024)S(1)} %copy-done.2, f32[128]{0:T(128)S(1)} %slice_bitcast_fusion), kind=kLoop, calls=%fused_computation.1 | loop fusion | flops 1048576 | bytes 1057280 | tf_op jit(solution)/shard_map/reshape | solution.py:353
  (4 shorter events, 0.0 us)
Async XLA Ops:
  0.0 5.3 %copy-start.1 = (bf16[1,128,2,512]{3,2,1,0:T(2,128)(2,1)S(1)}, bf16[1,128,2,512]{3,2,1,0:T(2,128)(2,1)}, u32[]{:S(2)}) copy-start(bf16[1,128,2,512]{3,2,1,0:T(2,128)(2,1)} %param.9) | copy-start | bytes 786436
  0.0 5.3 %copy-start = (bf16[1,128,2048]{2,1,0:T(8,128)(2,1)S(1)}, bf16[1,128,2048]{2,1,0:T(8,128)(2,1)}, u32[]{:S(2)}) copy-start(bf16[1,128,2048]{2,1,0:T(8,128)(2,1)} %param.8) | copy-start | bytes 1572868
  5.3 46.7 %copy-start.2 = (f32[2048]{0:T(1024)S(1)}, f32[2048]{0:T(1024)}, u32[]{:S(2)}) copy-start(f32[2048]{0:T(1024)} %param.13) | copy-start | bytes 24580

commit v3 on v2

--- a/solution.py
+++ b/solution.py
@@ -12,15 +12,16 @@
 BLOCK = 8
 EPSILON = 1e-05
 LANES = 128
+WINDOW = 3
 ROW_KEY = 1024.0
 MESH = pl.DeviceIdType.MESH
 
 
 def kernel(
     n_phase, n_tensor, total_features,
-    x_ref, bc_ref, dt_ref, head_ref, meta_ref,
+    x_ref, bc_ref, dt_ref, decay_ref, direct_ref, routes_ref, seg_ref,
     y_ref, scale_ref,
-    xall, bcall, dtall, meta, metaprev, local, xscaled, hin, hout, ysend, ymine, sums, mysum,
+    xall, bcall, dtall, mymeta, meta, metaprev, local, xscaled, hin, hout, ysend, ymine, sums, mysum,
     s_meta, r_meta, s_dt, r_dt, s_bc, r_bc, s_x, r_x, s_h, r_h, s_y, r_y, s_sum, r_sum, s_own,
 ):
     f32, bf16 = jnp.float32, jnp.bfloat16
@@ -30,7 +31,9 @@
     half = width // 2
     chunks = half // LANES
     n = STATE_ENTRIES
-    heads = dt_ref.shape[1]
+    blocks = dt_ref.shape[0]
+    heads = decay_ref.shape[1] // 2
+    lanes_dt = heads * BLOCK
     partner = (other, phase, place)
     first = phase == 0
 
@@ -45,6 +48,16 @@
     )
     own_x.start()
 
+    token_block = lax.broadcasted_iota(jnp.int32, (blocks, tok), 1) // BLOCK
+    widen = jnp.where(token_block == lax.broadcasted_iota(jnp.int32, (blocks, tok), 0), 1.0, 0.0)
+    own_rows = jnp.dot(
+        jnp.broadcast_to(routes_ref[...].astype(f32), (8, blocks)).astype(bf16),
+        widen.astype(bf16), preferred_element_type=f32,
+    )
+    mymeta[...] = own_rows
+    for j in range(2):
+        mymeta[2 + j : 3 + j, :] = seg_ref[0:1, j * tok : (j + 1) * tok].astype(f32)
+
     barrier = pltpu.get_barrier_semaphore()
     pl.semaphore_signal(barrier, inc=1, device_id=partner, device_id_type=MESH)
     for k in range(1, n_tensor):
@@ -72,8 +85,11 @@
         )
 
     copies = [
-        remote(meta_ref, meta.at[me], s_meta.at[0], r_meta.at[0], partner),
-        remote(dt_ref.at[other], dtall.at[me], s_dt, r_dt, partner),
+        remote(mymeta, meta.at[me], s_meta.at[0], r_meta.at[0], partner),
+        remote(
+            dt_ref.at[:, pl.ds(pl.multiple_of(other * lanes_dt, LANES), lanes_dt)],
+            dtall.at[me], s_dt, r_dt, partner,
+        ),
         remote(bc_ref.at[:, other_group], bcall.at[my_rows, pl.ds(0, n)], s_bc.at[0], r_bc.at[0], partner),
         remote(bc_ref.at[:, other_c], bcall.at[my_rows, pl.ds(n, n)], s_bc.at[1], r_bc.at[1], partner),
     ]
@@ -87,7 +103,7 @@
     ]
     after = jnp.minimum(phase + 1, n_phase - 1)
     ahead = [
-        remote(meta_ref, metaprev.at[me], s_meta.at[1 + i], r_meta.at[1 + i], (d, after, place))
+        remote(mymeta, metaprev.at[me], s_meta.at[1 + i], r_meta.at[1 + i], (d, after, place))
         for i, d in enumerate((me, other))
     ]
     h_copies = [
@@ -100,7 +116,8 @@
         ]
         for c in range(chunks)
     ]
-    for copy in copies[:3] + x_copies[:4] + copies[3:] + x_copies[4:]:
+    queue = x_copies + copies[3:]
+    for copy in copies[:3] + queue[:2]:
         copy.start()
 
     @pl.when(phase < n_phase - 1)
@@ -108,8 +125,8 @@
         for copy in ahead:
             copy.start()
 
-    meta[me] = meta_ref[...]
-    dtall[me] = dt_ref[me]
+    meta[me] = mymeta[...]
+    dtall[me] = dt_ref[:, pl.ds(pl.multiple_of(me * lanes_dt, LANES), lanes_dt)]
     bcall[my_rows, pl.ds(0, n)] = bc_ref[:, my_group]
     bcall[my_rows, pl.ds(n, n)] = bc_ref[:, my_c]
 
@@ -122,15 +139,38 @@
     at_row = lax.broadcasted_iota(jnp.int32, (both, both), 0)
     at_col = lax.broadcasted_iota(jnp.int32, (both, both), 1)
     causal = at_row >= at_col
-    unit = jnp.where(at_row == at_col, 1.0, 0.0).astype(bf16)
-    slots = lax.broadcasted_iota(jnp.int32, (tok, tok), 0).astype(f32)
+    tok_row = lax.broadcasted_iota(jnp.int32, (tok, tok), 0)
+    tok_col = lax.broadcasted_iota(jnp.int32, (tok, tok), 1)
+    before = tok_row // BLOCK < tok_col // BLOCK
+    inner = (tok_col % BLOCK)[0:1].astype(f32)
+    widen_t = jnp.where(
+        lax.broadcasted_iota(jnp.int32, (tok, blocks), 0) // BLOCK
+        == lax.broadcasted_iota(jnp.int32, (tok, blocks), 1),
+        1.0, 0.0,
+    ).astype(bf16)
+    same_place = (
+        lax.broadcasted_iota(jnp.int32, (tok, lanes_dt), 0) % BLOCK
+        == lax.broadcasted_iota(jnp.int32, (tok, lanes_dt), 1) % BLOCK
+    )
+    gather_head = jnp.where(
+        lax.broadcasted_iota(jnp.int32, (lanes_dt, LANES), 0) // BLOCK
+        == lax.broadcasted_iota(jnp.int32, (lanes_dt, LANES), 1),
+        1.0, 0.0,
+    ).astype(bf16)
+    slots = tok_row.astype(f32)
 
     copies[0].wait_recv()
 
     row_lanes, key_lanes, row_subl, key_subl = [], [], [], []
     for j in range(2):
         rows = meta[j, 0:1, :]
-        places = jnp.where(slots == meta[j, 1:2, :], 1.0, 0.0).astype(bf16)
+        rows_t = jnp.broadcast_to(rows, (tok, tok)).T
+        count = jnp.dot(
+            jnp.ones((8, tok), bf16),
+            jnp.where(before & (rows_t == rows), 1.0, 0.0).astype(bf16),
+            preferred_element_type=f32,
+        )
+        places = jnp.where(slots == count[0:1] + inner, 1.0, 0.0).astype(bf16)
         found = [
             jnp.dot(meta[d].astype(bf16), places, preferred_element_type=f32)[2 + j : 3 + j, :]
             for d in range(2)
@@ -138,7 +178,7 @@
         key = rows * ROW_KEY + jnp.where(rows == 0.0, found[0], found[1])
         row_lanes.append(rows)
         key_lanes.append(key)
-        row_subl.append(jnp.broadcast_to(rows, (tok, tok)).T)
+        row_subl.append(rows_t)
         key_subl.append(jnp.broadcast_to(key, (tok, tok)).T)
     row_lane, key_lane = jnp.concatenate(row_lanes, 1), jnp.concatenate(key_lanes, 1)
     row_sub, key_sub = jnp.concatenate(row_subl, 0), jnp.concatenate(key_subl, 0)
@@ -151,18 +191,32 @@
     ends = [meta[d, 3:4, tok - 1 : tok] for d in range(2)]
 
     copies[1].wait_recv()
-    decay = head_ref[me, 0:1, 0:heads]
-    dt_lanes = jnp.concatenate([dtall[0], dtall[1]], 1)
-    steps = lax.dot_general(
-        jnp.concatenate([same_row, unit, picks], 0), dt_lanes,
-        (((1,), (1,)), ((), ())), preferred_element_type=f32,
+    decay, direct_w = [
+        jnp.concatenate(
+            [
+                jnp.where(me == 0, ref[0:1, 0:heads], ref[0:1, heads : 2 * heads]),
+                jnp.zeros((1, LANES - heads), f32),
+            ],
+            1,
+        )
+        for ref in (decay_ref, direct_ref)
+    ]
+    dt_parts = []
+    for j in range(2):
+        wide = jnp.dot(widen_t, dtall[j], preferred_element_type=f32)
+        wide = jnp.where(same_place, wide, 0.0).astype(bf16)
+        dt_parts.append(jnp.dot(wide, gather_head, preferred_element_type=f32))
+    dt = jnp.concatenate(dt_parts, 0)
+    steps = jnp.dot(
+        jnp.concatenate([same_row, picks], 0), dt.astype(bf16), preferred_element_type=f32
     )
     log_decay = -decay * steps[0:both]
-    grow = jnp.exp(-log_decay) * steps[both : 2 * both]
+    grow = jnp.exp(-log_decay) * dt
     shrink = jnp.exp(log_decay)
-    whole = jnp.exp(-decay * steps[2 * both : 2 * both + 8])
+    whole = jnp.exp(-decay * steps[both : both + 8])
 
     copies[2].wait_recv()
+    queue[2].start()
     b_mat = bcall[:, 0:n]
     b_float = b_mat.astype(f32)
     b_both_t = jnp.concatenate(
@@ -182,9 +236,12 @@
             jnp.broadcast_to(a[:, 2 * c + 1 : 2 * c + 2], shape),
         )
 
+    pieces = [copy for pair in h_copies for copy in pair]
     own_x.wait()
     for c in range(chunks):
         x_copies[c].wait_recv()
+        if c + 3 < len(queue):
+            queue[c + 3].start()
         cols = pl.ds(c * LANES, LANES)
         scaled = (xall[:, cols].astype(f32) * spread(grow, c)).astype(bf16)
         xscaled[:, cols] = scaled
@@ -198,6 +255,8 @@
         def _():
             hout[c] = update.astype(bf16)
             for d in range(2):
+                if 2 * c + d >= WINDOW:
+                    pieces[2 * c + d - WINDOW].wait_send()
                 h_copies[c][d].start()
 
         @pl.when(phase > 0)
@@ -230,7 +289,7 @@
         cols = pl.ds(c * LANES, LANES)
         inside = jnp.dot(scores, xscaled[:, cols], preferred_element_type=f32)
         decayed = spread(shrink, c)
-        direct = spread(head_ref[me, 1:2, :], c) * xall[:, cols].astype(f32)
+        direct = spread(direct_w, c) * xall[:, cols].astype(f32)
         keep = spread(whole, c)
         for d in range(2):
             rows = pl.ds(d * n, n)
@@ -281,7 +340,12 @@
 
     @pl.when(phase < n_phase - 1)
     def _():
-        for copy in ahead + [copy for pair in h_copies for copy in pair]:
+        for copy in ahead + pieces[-WINDOW:]:
+            copy.wait_send()
+
+    @pl.when((phase > 0) & (phase < n_phase - 1))
+    def _():
+        for copy in pieces[:-WINDOW]:
             copy.wait_send()
 
     for k in range(1, n_tensor):
@@ -304,18 +368,6 @@
     n = STATE_ENTRIES
     f32, bf16 = jnp.float32, jnp.bfloat16
 
-    targets = routes[0, :, 0]
-    order = jnp.arange(blocks)
-    earlier = order[:, None] > order[None, :]
-    rank = jnp.sum((targets[:, None] == targets[None, :]) & earlier, axis=1)
-    row = jnp.broadcast_to(targets[:, None], (blocks, BLOCK)).reshape(1, tok)
-    slot = (rank[:, None] * BLOCK + jnp.arange(BLOCK)[None, :]).reshape(1, tok)
-    meta = jnp.concatenate(
-        [row, slot, segments.reshape(2, tok), jnp.zeros((4, tok), jnp.int32)], 0
-    ).astype(f32)
-    dt = step_sizes.reshape(blocks, 2, heads, BLOCK).transpose(1, 2, 0, 3).reshape(2, heads, tok)
-    by_head = jnp.stack([decay_rates.reshape(2, heads), direct_weight.reshape(2, heads)], 1)
-    by_head = jnp.pad(by_head, ((0, 0), (0, 6), (0, LANES - heads)))
     dma = pltpu.SemaphoreType.DMA
     vmem = pltpu.VMEM
     y, scale = pl.pallas_call(
@@ -325,12 +377,13 @@
             jax.ShapeDtypeStruct((8, tok), f32),
         ],
         in_specs=[pl.BlockSpec(memory_space=pltpu.HBM)]
-        + [pl.BlockSpec(memory_space=pltpu.VMEM)] * 4,
+        + [pl.BlockSpec(memory_space=pltpu.VMEM)] * 6,
         out_specs=[pl.BlockSpec(memory_space=pltpu.VMEM)] * 2,
         scratch_shapes=[
             vmem((2 * tok, half), bf16),
             vmem((2 * tok, 2 * n), bf16),
-            vmem((2, heads, tok), bf16),
+            vmem((2, blocks, heads * BLOCK), bf16),
+            vmem((8, tok), f32),
             vmem((2, 8, tok), f32),
             vmem((2, 8, tok), f32),
             vmem((chunks, 2 * n, LANES), f32),
@@ -348,7 +401,10 @@
         compiler_params=pltpu.CompilerParams(
             collective_id=0, has_side_effects=True, vmem_limit_bytes=40 * 2**20
         ),
-    )(tokens.reshape(tok, width), bc_proj.reshape(tok, -1), dt, by_head, meta)
+    )(
+        tokens.reshape(tok, width), bc_proj.reshape(tok, -1), step_sizes.reshape(blocks, -1),
+        decay_rates.reshape(1, -1), direct_weight.reshape(1, -1), routes.reshape(1, -1), segments,
+    )
     mixed = y.astype(f32) * scale[0][:, None] * norm_gain[None, :]
     return mixed.astype(bf16).reshape(1, tok, width)
 

time: 53.2 us -> 50.5 us (0.949)
  local copies, waits for them, and re-layouts: 3.54 us -> 1.73 us
  other arithmetic: 2.75 us -> 0.98 us
  Pallas kernels: 46.7 us -> 47.6 us
    another operation x2 -> x0, local copies, waits for them, and re-layouts: 1.47 us -> none  [per_device(): jnp.stack([decay_rates.reshape(2, heads), direct_weight.reshape(2, heads)...]
    pallas_call x1, Pallas kernels: 46.7 us -> 47.6 us  [per_device(): pl.pallas_call(functools.partial(kernel, n_phase, n_tensor, float(n_tenso...]
    reduce_sum x1 -> x0, other arithmetic: 0.93 us -> none  [per_device(): rank = jnp.sum((targets[:, None] == targets[None, :]) & earlier, axis=1)]
    unnamed x8 -> x15, local copies, waits for them, and re-layouts: 0.88 us -> 1.72 us
    convert_element_type x1 -> x0, other arithmetic: 0.75 us -> none  [per_device(): meta = jnp.concatenate([row, slot, segments.reshape(2, tok), jnp.zeros((4...]
    broadcast_in_dim x2 -> x0, local copies, waits for them, and re-layouts: 0.73 us -> none  [the longest x1 0.73 us: per_device(): row = jnp.broadcast_to(targets[:, None], (blocks, BLOCK)).reshape(1, tok)]
where the time goes in v3:
time: 50.5 us; the launch traced here: 50.4 us
  Pallas kernels  47.6 us (94%)
  local copies, waits for them, and re-layouts  1.73 us (3%)
  other arithmetic  0.98 us (2%)
    pallas_call x1, Pallas kernels, per_device(): pl.pallas_call(functools.partial(kernel, n_phase, n_tensor, float(n_tenso...  47.6 us
    unnamed x15, local copies, waits for them, and re-layouts  1.72 us

profile of v3, /device:TPU:25, one launch (start us, length us, event | category | flops | bytes accessed | tf_op | source)
XLA Modules:
  0.0 50.4 jit_solution(11264058181277734418)
XLA Ops:
  0.0 0.0 copy-start
  0.0 0.0 copy-start.1
  0.0 0.0 copy-start.4
  0.0 0.0 copy-start.5
  0.0 1.0 %copy.9 = bf16[16,8,2,512]{3,1,2,0:T(8,128)(2,1)S(1)} copy(bf16[16,8,2,512]{3,2,1,0:T(2,128)(2,1)} %bitcast.18) | data formatting | bytes 524288
  1.1 0.0 copy-start.2
  1.1 0.0 copy-start.3
  1.1 0.0 copy-done
  1.1 0.0 copy-done.1
  1.1 0.0 copy-done.4
  1.1 0.0 copy-done.5
  1.1 0.6 %copy-done.2 = s32[1,256]{1,0:T(1,128)S(1)} copy-done((s32[1,256]{1,0:T(1,128)S(1)}, s32[1,256]{1,0:T(1,128)}, u32[]{:S(2)}) %copy-start.2) | copy-done | bytes 1048
  1.8 0.0 copy-done.3
  1.8 0.0 copy-start.6
  1.8 47.6 %shard_map.82 = (bf16[128,2048]{1,0:T(8,128)(2,1)S(1)}, f32[8,128]{1,0:T(8,128)S(1)}) custom-call(bf16[128,2048]{1,0:T(8,128)(2,1)S(1)} %bitcast.13, bf16[128,1024]{1,0:T(8,128)(2,1)S(1)} %bitcast.12, bf16[16,256]{1,0:T(8,128)(2,1)S(1)} %bitcast.14, f32[1,32]{1,0:T(1,128)S(1)} %bitcast.15, f32[1,32]{1,0:T(1,128)S(1)} %bitcast.16, s32[1,16]{1,0:T(1,128)S(1)} %bitcast.17, ...), custom_call_target="tpu_custom_call" | custom-call | tf_op jit(solution)/shard_map/pallas_call | solution.py:373
  49.4 0.0 copy-done.6
  49.4 1.0 %fusion = bf16[1,128,2048]{2,1,0:T(8,128)(2,1)} fusion(bf16[128,2048]{1,0:T(8,128)(2,1)S(1)} %get-tuple-element.7, f32[2048]{0:T(1024)S(1)} %copy-done.6, f32[128]{0:T(128)S(1)} %slice_bitcast_fusion), kind=kLoop, calls=%fused_computation.1 | loop fusion | flops 1048576 | bytes 1057280 | tf_op jit(solution)/shard_map/reshape | solution.py:409
  (1 shorter events, 0.0 us)
Async XLA Ops:
  0.0 1.1 %copy-start = (bf16[1,128,2048]{2,1,0:T(8,128)(2,1)S(1)}, bf16[1,128,2048]{2,1,0:T(8,128)(2,1)}, u32[]{:S(2)}) copy-start(bf16[1,128,2048]{2,1,0:T(8,128)(2,1)} %param.8) | copy-start | bytes 1572868
  0.0 1.1 %copy-start.1 = (bf16[1,16,256]{2,1,0:T(8,128)(2,1)S(1)}, bf16[1,16,256]{2,1,0:T(8,128)(2,1)}, u32[]{:S(2)}) copy-start(bf16[1,16,256]{2,1,0:T(8,128)(2,1)} %param.10) | copy-start | bytes 24580
  0.0 1.1 %copy-start.4 = (f32[32]{0:T(128)S(1)}, f32[32]{0:T(128)}, u32[]{:S(2)}) copy-start(f32[32]{0:T(128)} %param.12) | copy-start | bytes 388
  0.0 1.1 %copy-start.5 = (s32[1,16,1]{1,2,0:T(1,128)S(1)}, s32[1,16,1]{1,2,0:T(1,128)}, u32[]{:S(2)}) copy-start(s32[1,16,1]{1,2,0:T(1,128)} %param.14) | copy-start | bytes 196
  1.1 0.7 %copy-start.2 = (s32[1,256]{1,0:T(1,128)S(1)}, s32[1,256]{1,0:T(1,128)}, u32[]{:S(2)}) copy-start(s32[1,256]{1,0:T(1,128)} %seg_ref.1) | copy-start | bytes 3076
  1.1 0.7 %copy-start.3 = (f32[32]{0:T(128)S(1)}, f32[32]{0:T(128)}, u32[]{:S(2)}) copy-start(f32[32]{0:T(128)} %param.11) | copy-start | bytes 388
  1.8 47.6 %copy-start.6 = (f32[2048]{0:T(1024)S(1)}, f32[2048]{0:T(1024)}, u32[]{:S(2)}) copy-start(f32[2048]{0:T(1024)} %param.13) | copy-start | bytes 24580

commit v4 on v3

--- a/solution.py
+++ b/solution.py
@@ -116,7 +116,7 @@
         ]
         for c in range(chunks)
     ]
-    queue = x_copies + copies[3:]
+    queue = x_copies[:2] + copies[3:] + x_copies[2:]
     for copy in copies[:3] + queue[:2]:
         copy.start()
 
@@ -217,6 +217,7 @@
 
     copies[2].wait_recv()
     queue[2].start()
+    queue[3].start()
     b_mat = bcall[:, 0:n]
     b_float = b_mat.astype(f32)
     b_both_t = jnp.concatenate(
@@ -237,11 +238,53 @@
         )
 
     pieces = [copy for pair in h_copies for copy in pair]
+
+    @pl.when(phase > 0)
+    def _():
+        for copy in ahead:
+            copy.wait_recv()
+
+    befores = [metaprev[d, 3:4, tok - 1 : tok] for d in range(2)]
+    through = [jnp.where(ends[d] == befores[d], 1.0, 0.0) for d in range(2)]
     own_x.wait()
+
+    def mixers():
+        copies[3].wait_recv()
+        c_mat = bcall[:, n : 2 * n]
+        c_float = c_mat.astype(f32)
+        c_both = jnp.concatenate(
+            [
+                jnp.where(key_sub2 == befores[d] + d * ROW_KEY, c_float, 0.0).astype(bf16)
+                for d in range(2)
+            ],
+            1,
+        )
+        scores = lax.dot_general(c_mat, b_mat, (((1,), (1,)), ((), ())), preferred_element_type=f32)
+        scores = jnp.where(causal & (key_sub2 == key_lane), scores, 0.0).astype(bf16)
+        return scores, c_both
+
+    def output(c, scores, c_both, squares):
+        cols = pl.ds(c * LANES, LANES)
+        inside = jnp.dot(scores, xscaled[:, cols], preferred_element_type=f32)
+        carried = jnp.dot(c_both, hin[c], preferred_element_type=f32)
+        direct = spread(direct_w, c) * xall[:, cols].astype(f32)
+        ysend[c] = (spread(shrink, c) * (inside + carried) + direct).astype(bf16)
+        here = pl.ds(pl.multiple_of(me * half + c * LANES, LANES), LANES)
+        copy = remote(ysend.at[c, other_rows], ymine.at[:, here], s_y.at[c], r_y.at[c], partner)
+        copy.start()
+        y_copies.append(copy)
+        own = ysend[c, my_rows]
+        y_ref[:, here] = own
+        own = own.astype(f32)
+        return squares + own * own
+
+    squares = jnp.zeros((tok, LANES), f32)
+    y_copies = []
+    scores = c_both = None
     for c in range(chunks):
         x_copies[c].wait_recv()
-        if c + 3 < len(queue):
-            queue[c + 3].start()
+        if c + 4 < len(queue):
+            queue[c + 4].start()
         cols = pl.ds(c * LANES, LANES)
         scaled = (xall[:, cols].astype(f32) * spread(grow, c)).astype(bf16)
         xscaled[:, cols] = scaled
@@ -259,38 +302,14 @@
                     pieces[2 * c + d - WINDOW].wait_send()
                 h_copies[c][d].start()
 
-        @pl.when(phase > 0)
+        @pl.when((phase > 0) & (phase < n_phase - 1))
         def _():
             local[c] = update
 
-    @pl.when(phase > 0)
-    def _():
-        for copy in ahead:
-            copy.wait_recv()
-
-    befores = [metaprev[d, 3:4, tok - 1 : tok] for d in range(2)]
-    through = [jnp.where(ends[d] == befores[d], 1.0, 0.0) for d in range(2)]
-    copies[3].wait_recv()
-    c_mat = bcall[:, n : 2 * n]
-    c_float = c_mat.astype(f32)
-    c_both = jnp.concatenate(
-        [
-            jnp.where(key_sub2 == befores[d] + d * ROW_KEY, c_float, 0.0).astype(bf16)
-            for d in range(2)
-        ],
-        1,
-    )
-    scores = lax.dot_general(c_mat, b_mat, (((1,), (1,)), ((), ())), preferred_element_type=f32)
-    scores = jnp.where(causal & (key_sub2 == key_lane), scores, 0.0).astype(bf16)
-
-    squares = jnp.zeros((tok, LANES), f32)
-    y_copies = []
-    for c in range(chunks):
-        cols = pl.ds(c * LANES, LANES)
-        inside = jnp.dot(scores, xscaled[:, cols], preferred_element_type=f32)
-        decayed = spread(shrink, c)
-        direct = spread(direct_w, c) * xall[:, cols].astype(f32)
-        keep = spread(whole, c)
+        if c == 1:
+            scores, c_both = mixers()
+        if c > 0:
+            squares = output(c - 1, scores, c_both, squares)
         for d in range(2):
             rows = pl.ds(d * n, n)
 
@@ -305,16 +324,7 @@
                 ).astype(bf16)
                 h_copies[c][d].start()
 
-        carried = jnp.dot(c_both, hin[c], preferred_element_type=f32)
-        ysend[c] = (decayed * (inside + carried) + direct).astype(bf16)
-        here = pl.ds(pl.multiple_of(me * half + c * LANES, LANES), LANES)
-        copy = remote(ysend.at[c, other_rows], ymine.at[:, here], s_y.at[c], r_y.at[c], partner)
-        copy.start()
-        y_copies.append(copy)
-        own = ysend[c, my_rows]
-        y_ref[:, here] = own
-        own = own.astype(f32)
-        squares = squares + own * own
+    squares = output(chunks - 1, scores, c_both, squares)
 
     for c in range(chunks):
         y_copies[c].wait_recv()

time: 50.5 us -> 46 us (0.911)
  Pallas kernels: 47.6 us -> 43.1 us
    pallas_call x1, Pallas kernels: 47.6 us -> 43.1 us  [per_device(): pl.pallas_call(functools.partial(kernel, n_phase, n_tensor, float(n_tenso...]
where the time goes in v4:
time: 46 us; the launch traced here: 45.8 us
  Pallas kernels  43.1 us (94%)
  local copies, waits for them, and re-layouts  1.73 us (4%)
  other arithmetic  0.98 us (2%)
    pallas_call x1, Pallas kernels, per_device(): pl.pallas_call(functools.partial(kernel, n_phase, n_tensor, float(n_tenso...  43.1 us
    unnamed x15, local copies, waits for them, and re-layouts  1.72 us
    reshape x1, other arithmetic, per_device(): return mixed.astype(bf16).reshape(1, tok, width)  0.98 us

profile of v4, /device:TPU:25, one launch (start us, length us, event | category | flops | bytes accessed | tf_op | source)
XLA Modules:
  0.0 45.8 jit_solution(1857322253452133876)
XLA Ops:
  0.0 0.0 copy-start
  0.0 0.0 copy-start.1
  0.0 0.0 copy-start.4
  0.0 0.0 copy-start.5
  0.0 1.0 %copy.9 = bf16[16,8,2,512]{3,1,2,0:T(8,128)(2,1)S(1)} copy(bf16[16,8,2,512]{3,2,1,0:T(2,128)(2,1)} %bitcast.18) | data formatting | bytes 524288
  1.1 0.0 copy-start.2
  1.1 0.0 copy-start.3
  1.1 0.0 copy-done
  1.1 0.0 copy-done.1
  1.1 0.0 copy-done.4
  1.1 0.0 copy-done.5
  1.1 0.6 %copy-done.2 = s32[1,256]{1,0:T(1,128)S(1)} copy-done((s32[1,256]{1,0:T(1,128)S(1)}, s32[1,256]{1,0:T(1,128)}, u32[]{:S(2)}) %copy-start.2) | copy-done | bytes 1048
  1.8 0.0 copy-done.3
  1.8 0.0 copy-start.6
  1.8 43.1 %shard_map.82 = (bf16[128,2048]{1,0:T(8,128)(2,1)S(1)}, f32[8,128]{1,0:T(8,128)S(1)}) custom-call(bf16[128,2048]{1,0:T(8,128)(2,1)S(1)} %bitcast.13, bf16[128,1024]{1,0:T(8,128)(2,1)S(1)} %bitcast.12, bf16[16,256]{1,0:T(8,128)(2,1)S(1)} %bitcast.14, f32[1,32]{1,0:T(1,128)S(1)} %bitcast.15, f32[1,32]{1,0:T(1,128)S(1)} %bitcast.16, s32[1,16]{1,0:T(1,128)S(1)} %bitcast.17, ...), custom_call_target="tpu_custom_call" | custom-call | tf_op jit(solution)/shard_map/pallas_call | solution.py:383
  44.8 0.0 copy-done.6
  44.9 1.0 %fusion = bf16[1,128,2048]{2,1,0:T(8,128)(2,1)} fusion(bf16[128,2048]{1,0:T(8,128)(2,1)S(1)} %get-tuple-element.7, f32[2048]{0:T(1024)S(1)} %copy-done.6, f32[128]{0:T(128)S(1)} %slice_bitcast_fusion), kind=kLoop, calls=%fused_computation.1 | loop fusion | flops 1048576 | bytes 1057280 | tf_op jit(solution)/shard_map/reshape | solution.py:419
  (1 shorter events, 0.0 us)
Async XLA Ops:
  0.0 1.1 %copy-start = (bf16[1,128,2048]{2,1,0:T(8,128)(2,1)S(1)}, bf16[1,128,2048]{2,1,0:T(8,128)(2,1)}, u32[]{:S(2)}) copy-start(bf16[1,128,2048]{2,1,0:T(8,128)(2,1)} %param.8) | copy-start | bytes 1572868
  0.0 1.1 %copy-start.1 = (bf16[1,16,256]{2,1,0:T(8,128)(2,1)S(1)}, bf16[1,16,256]{2,1,0:T(8,128)(2,1)}, u32[]{:S(2)}) copy-start(bf16[1,16,256]{2,1,0:T(8,128)(2,1)} %param.10) | copy-start | bytes 24580
  0.0 1.1 %copy-start.4 = (f32[32]{0:T(128)S(1)}, f32[32]{0:T(128)}, u32[]{:S(2)}) copy-start(f32[32]{0:T(128)} %param.12) | copy-start | bytes 388
  0.0 1.1 %copy-start.5 = (s32[1,16,1]{1,2,0:T(1,128)S(1)}, s32[1,16,1]{1,2,0:T(1,128)}, u32[]{:S(2)}) copy-start(s32[1,16,1]{1,2,0:T(1,128)} %param.14) | copy-start | bytes 196
  1.1 0.7 %copy-start.2 = (s32[1,256]{1,0:T(1,128)S(1)}, s32[1,256]{1,0:T(1,128)}, u32[]{:S(2)}) copy-start(s32[1,256]{1,0:T(1,128)} %seg_ref.1) | copy-start | bytes 3076
  1.1 0.7 %copy-start.3 = (f32[32]{0:T(128)S(1)}, f32[32]{0:T(128)}, u32[]{:S(2)}) copy-start(f32[32]{0:T(128)} %param.11) | copy-start | bytes 388
  1.8 43.1 %copy-start.6 = (f32[2048]{0:T(1024)S(1)}, f32[2048]{0:T(1024)}, u32[]{:S(2)}) copy-start(f32[2048]{0:T(1024)} %param.13) | copy-start | bytes 24580
